TPU v7x, 128 devices: a whole 4x4x4 slice. The times are simulated.
128 devices in a mesh: rep: 16 (over x_hi, z, core), shard: 8 (over y, x_lo).
Axes of the slice: x: 4 (x_hi: 2, x_lo: 2; x = x_hi * 2 + x_lo), y: 4, z: 4, core: 2. Of those that a mesh axis runs over, the one named last changes fastest.
Arguments:
- anchor: bfloat16 [8, 256, 3072], P('shard'), may hold values from -4 to 4
- local_params: bfloat16 [16, 8, 256, 3072], P('rep', 'shard'), may hold values from -6 to 6
- momentum: float32 [8, 256, 3072], P('shard', 'rep'), may hold values from -4 to 4
- out_grad: bfloat16 [16, 1024, 3072], P('rep', 'shard'), may hold values from -4 to 4
- pre_act: bfloat16 [16, 1024, 12288], P('rep', None, 'shard'), may hold values from -6 to 6
- down_weight: bfloat16 [16, 12288, 3072], P('rep', 'shard'), may hold values from -0.0546875 to 0.0546875
Outputs:
- new_anchor: bfloat16 [8, 256, 3072], P('shard')
- new_momentum: float32 [8, 256, 3072], P('shard', 'rep')
- pre_grad: bfloat16 [16, 1024, 12288], P('rep', None, 'shard')
- weight_grad: bfloat16 [16, 12288, 3072], P('rep', 'shard')
All inputs are finite; a program needn't handle non-finite values. Where the computation divides by a largest or mean magnitude, that divisor is 1e-20 or more.
Results may differ from a plain program's by a relative error of at most 0.0069.
Values may be sent and summed in bfloat16 or wider, within the bound.
No kernel may reach another device: no remote copies, remote signals or barrier semaphores. Data moves between devices by JAX's collectives and lax.ppermute only.
A program may use at most 128 MiB of HBM per device.

v0:
```python
import jax
import jax.numpy as jnp
from jax import lax
from jax.sharding import PartitionSpec as P

BLOCK = 128


epsilon = 1e-06
outer_beta = 0.9
outer_rate = 0.7


def encode(values):
    layout = values.shape
    blocks = values.reshape(layout[:-1] + (layout[-1] // BLOCK, BLOCK))
    scales = (jnp.max(jnp.abs(blocks), axis=-1) + epsilon).astype(jnp.bfloat16)
    scales = lax.optimization_barrier(scales)
    coded = (blocks / scales.astype(jnp.float32)[..., None]).astype(jnp.bfloat16)
    coded = lax.optimization_barrier(coded)
    return (coded.reshape(layout), scales)


def decode(coded, scales):
    layout = coded.shape
    blocks = coded.astype(jnp.float32).reshape(layout[:-1] + (layout[-1] // BLOCK, BLOCK))
    return (blocks * scales.astype(jnp.float32)[..., None]).reshape(layout)


def shards(anchor, local_params, momentum, out_grad, pre_act, down_weight):
    pre_rows = pre_act[0]
    weight = down_weight[0]
    hidden = jax.nn.gelu(pre_rows.astype(jnp.float32)).astype(jnp.bfloat16)
    grad_rows = lax.all_gather(out_grad, "shard", axis=1, tiled=True)[0]
    weight_sum = lax.dot_general(
        hidden, grad_rows, (((0,), (0,)), ((), ())), preferred_element_type=jnp.float32
    )
    hidden_grad = lax.dot_general(
        grad_rows, weight, (((1,), (1,)), ((), ())), preferred_element_type=jnp.float32
    )
    saved_rows = pre_rows.astype(jnp.float32)
    _, pullback = jax.vjp(jax.nn.gelu, saved_rows)
    new_slopes = pullback(hidden_grad)[0].astype(jnp.bfloat16)
    slopes = new_slopes
    weight_sum, slopes = (weight_sum, slopes)
    drift = anchor.astype(jnp.float32) - local_params[0].astype(jnp.float32)
    drift_code, drift_scale = encode(drift)
    replicas = lax.axis_size("rep")
    summed = lax.psum_scatter(
        decode(drift_code, drift_scale), "rep", scatter_dimension=1, tiled=True
    )
    outer_grad = summed / replicas
    new_momentum = outer_beta * momentum + outer_grad
    outer_step = outer_grad + outer_beta * new_momentum
    step_code, step_scale = encode(outer_step)
    whole_code, whole_scale = (
        lax.all_gather(step_code, "rep", axis=1, tiled=True),
        lax.all_gather(step_scale, "rep", axis=1, tiled=True),
    )
    new_anchor = (anchor.astype(jnp.float32) - outer_rate * decode(whole_code, whole_scale)).astype(
        jnp.bfloat16
    )
    return (new_anchor, new_momentum, slopes[None], weight_sum.astype(jnp.bfloat16)[None])


def solution(mesh):
    return jax.shard_map(
        shards,
        mesh=mesh,
        in_specs=(
            P("shard", None, None),
            P("rep", "shard", None, None),
            P("shard", "rep", None),
            P("rep", "shard", None),
            P("rep", None, "shard"),
            P("rep", "shard", None),
        ),
        out_specs=(
            P("shard", None, None),
            P("shard", "rep", None),
            P("rep", None, "shard"),
            P("rep", "shard", None),
        ),
        check_vma=False,
    )
```

profile of v0, /device:TPU:1, one launch (start us, length us, event | category | flops | bytes accessed | tf_op | source)
XLA Modules:
  0.0 310.5 jit_solution(12068769322860322383)
XLA Ops:
  7.2 0.0 reduce-scatter.2.cloned.1.call-start
  7.2 2.4 fusion.33
  9.6 0.6 copy.10
  10.2 0.9 fusion.37
  11.1 1.0 fusion.38
  12.1 0.0 copy-start
  12.1 1.0 convert_multiply_fusion.3
  13.1 1.9 reshape.156
  15.0 0.0 reduce-scatter.2.cloned.1.call-update
  15.1 0.0 all-gather.3.cloned.1.call-start
  15.1 77.6 %reduce-scatter.2.cloned.1.call-done = f32[1,16,3072]{2,1,0:T(8,128)} async-done(((f32[1,256,3072]{2,1,0:T(8,128)}), f32[1,16,3072]{2,1,0:T(8,128)}) %reduce-scatter.2.cloned.1.call-update) | async-done | bytes 196624 | tf_op jit(solution)/shard_map/reduce_scatter | solution.py:49
  92.7 0.0 copy-done
  92.8 1.6 add_bitcast_fusion
  94.4 0.1 fusion.43
  94.6 0.1 fusion.44
  94.7 0.7 reshape.158
  95.4 0.0 all-gather.3.cloned.1.call-update
  95.4 0.0 all-gather.5.cloned.1.call-start
  95.5 0.7 all-gather.5.cloned.1.call-update
  96.2 23.4 %all_gather.10 = bf16[1,256,24]{2,1,0:T(8,128)(2,1)S(1)} all-gather(bf16[1,16,24]{2,1,0:T(8,128)(2,1)S(1)} %fusion.46), channel_id=1, replica_groups=mesh['rep'=16,'shard'=8] {'rep'}, dimensions={1}, use_global_device_ids=true | all-gather | bytes 13056 | tf_op jit(solution)/shard_map/all_gather | solution.py:58
  119.6 0.9 mul.102
  120.5 1.9 mul.103
  122.4 0.0 copy-start.2
  122.4 20.1 %all-gather.3.cloned.1.call-done = bf16[1,256,3072]{2,1,0:T(8,128)(2,1)} async-done(((bf16[1,16,3072]{2,1,0:T(8,128)(2,1)}), bf16[1,256,3072]{2,1,0:T(8,128)(2,1)}) %all-gather.3.cloned.1.call-update) | async-done | bytes 1572880 | tf_op jit(solution)/shard_map/all_gather | solution.py:57
  142.5 4.7 %fusion.34 = bf16[1,256,3072]{2,1,0:T(8,128)(2,1)} fusion(bf16[1,256,3072]{2,1,0:T(8,128)(2,1)} %param.6, f32[1,256,3072]{2,1,0:T(8,128)} %mul.103, bf16[1,256,3072]{2,1,0:T(8,128)(2,1)} %all-gather.3.cloned.1.call-done), kind=kLoop, calls=%fused_computation.34 | loop fusion | flops 4718592 | bytes 7864320 | tf_op jit(solution)/shard_map/convert_element_type | solution.py:60
  147.2 124.5 %all-gather.5.cloned.1.call-done = bf16[1,1024,3072]{2,1,0:T(8,128)(2,1)} async-done(((bf16[1,128,3072]{2,1,0:T(8,128)(2,1)}), bf16[1,1024,3072]{2,1,0:T(8,128)(2,1)}) %all-gather.5.cloned.1.call-update) | async-done | bytes 6291472 | tf_op jit(solution)/shard_map/all_gather | solution.py:34
  271.7 0.0 copy-done.2
  271.7 0.0 copy-start.1
  271.7 15.6 %fusion.4 = bf16[1,1536,3072]{2,1,0:T(8,128)(2,1)} fusion(bf16[1,1024,3072]{2,1,0:T(8,128)(2,1)} %all-gather.5.cloned.1.call-done, bf16[1,1024,1536]{2,1,0:T(8,128)(2,1)S(1)} %copy-done.2), kind=kOutput, calls=%fused_computation.10 | convolution fusion | flops 9684123648 | bytes 18874368 | tf_op jit(solution)/shard_map/dot_general | solution.py:35
  287.3 0.0 copy-done.1
  287.3 16.7 %fusion.28 = bf16[1,1024,1536]{2,1,0:T(8,128)(2,1)} fusion(bf16[1,1024,1536]{2,1,0:T(8,128)(2,1)S(1)} %copy-done.2, bf16[1,1536,3072]{2,1,0:T(8,128)(2,1)} %param.11, bf16[1,1024,3072]{2,1,0:T(8,128)(2,1)S(1)} %copy-done.1), kind=kOutput, calls=%fused_computation.32 | convolution fusion | flops 9696706560 | bytes 22020096 | tf_op jit(solution)/shard_map/dot_general | solution.py:38
  (6 shorter events, 0.1 us)
Async XLA Ops:
  7.2 85.6 %reduce-scatter.2.cloned.1.call-start = ((), (), s32[]{:S(2)}) async-start(), calls=%async_computation.1 | async-start | bytes 3342336 | tf_op jit(solution)/shard_map/reduce_scatter | solution.py:49
  12.1 80.6 %copy-start = (f32[1,16,3072]{2,1,0:T(8,128)S(1)}, f32[1,16,3072]{2,1,0:T(8,128)}, u32[]{:S(2)}) copy-start(f32[1,16,3072]{2,1,0:T(8,128)} %param.8) | copy-start | bytes 589828
  15.1 127.5 %all-gather.3.cloned.1.call-start = ((), (), s32[]{:S(2)}) async-start(), calls=%async_computation.2 | async-start | bytes 1671168 | tf_op jit(solution)/shard_map/all_gather | solution.py:57
  95.4 176.3 %all-gather.5.cloned.1.call-start = ((), (), s32[]{:S(2)}) async-start(), calls=%async_computation.3 | async-start | bytes 7077888 | tf_op jit(solution)/shard_map/all_gather | solution.py:34
  122.4 149.3 %copy-start.2 = (bf16[1,1024,1536]{2,1,0:T(8,128)(2,1)S(1)}, bf16[1,1024,1536]{2,1,0:T(8,128)(2,1)}, u32[]{:S(2)}) copy-start(bf16[1,1024,1536]{2,1,0:T(8,128)(2,1)} %param.10) | copy-start | bytes 9437188
  271.7 15.6 %copy-start.1 = (bf16[1,1024,3072]{2,1,0:T(8,128)(2,1)S(1)}, bf16[1,1024,3072]{2,1,0:T(8,128)(2,1)}, u32[]{:S(2)}) copy-start(bf16[1,1024,3072]{2,1,0:T(8,128)(2,1)} %all-gather.5.cloned.1.call-done) | copy-start | bytes 18874372
Sparse Core Ops, SparseCore 0:
  15.2 77.5 reduce-scatter.1
  95.8 46.6 all-gather.2
  144.2 127.4 all-gather.4
where the time goes:
time: 311 us
  waiting for transfers between devices  223 us (72%)
  matrix products  32.3 us (10%)
  blocking collectives  23.4 us (8%)
  between operations  13.8 us (4%)
  other arithmetic  11.8 us (4%)
  local copies, waits for them, and re-layouts  6 us (2%)
    all_gather x1, waiting for transfers between devices, shards(): grad_rows = lax.all_gather(out_grad, 'shard', axis=1, tiled=True)[0]  125 us
    reduce_scatter x1, waiting for transfers between devices, shards(): lax.psum_scatter(decode(drift_code, drift_scale), 'rep', scatter_dimensio...  77.6 us
    all_gather x1, blocking collectives, shards(): lax.all_gather(step_scale, 'rep', axis=1, tiled=True)  23.4 us
    all_gather x1, waiting for transfers between devices, shards(): lax.all_gather(step_code, 'rep', axis=1, tiled=True)  20.1 us
    dot_general x1, matrix products, shards(): lax.dot_general(grad_rows, weight, (((1,), (1,)), ((), ())), preferred_el...  16.7 us
    dot_general x1, matrix products, shards(): lax.dot_general(hidden, grad_rows, (((0,), (0,)), ((), ())), preferred_el...  15.6 us
  transfers between devices with their start and end apart: 3, of which 3 were waited for; matrix products, arithmetic and copies ran while one was open for 2% of the time, Pallas kernels for 0%

commit v1 on v0

v1 whole, which is shorter than its diff:
```python
import itertools

import jax
import jax.numpy as jnp
import numpy as np
from jax import lax
from jax.experimental import pallas as pl
from jax.experimental.pallas import tpu as pltpu
from jax.sharding import PartitionSpec as P

BLOCK = 128
D = 3072
FF = 1536
CHUNK = 128
ROWS = 16

epsilon = 1e-06
outer_beta = 0.9
outer_rate = 0.7

AXES = ("rep", "shard")
MIB = 1024 * 1024
PARTS = (48, 48, 32)


def device_index(xh, z, c, y, xl):
    return ((xh % 2 * 4 + z % 4) * 2 + c % 2) * 8 + y % 4 * 2 + xl % 2


def every_device():
    return itertools.product(range(2), range(4), range(2), range(4), range(2))


def shift(array, xh=0, z=0, c=0, y=0, xl=0):
    pairs = [
        (device_index(*at), device_index(at[0] + xh, at[1] + z, at[2] + c, at[3] + y, at[4] + xl))
        for at in every_device()
    ]
    return lax.ppermute(array, AXES, pairs)


def place_table():
    table = np.zeros((128, 12), np.int32)
    for at in every_device():
        xh, z, c, y, xl = at
        order = [(y, xl), (y - 1, xl), (y + 1, xl), (y, 1 - xl), (y + 1, 1 - xl), (y - 1, 1 - xl), (y + 2, xl), (y + 2, 1 - xl)]
        table[device_index(*at)] = [a % 4 * 2 + b for a, b in order] + [xh, z, c, (xh * 4 + z) * 2 + c]
    return table


def code_and_decode(values):
    scale = (jnp.max(jnp.abs(values), axis=-1, keepdims=True) + epsilon).astype(jnp.bfloat16).astype(jnp.float32)
    return (values / scale).astype(jnp.bfloat16).astype(jnp.float32) * scale


def drift_kernel(place, anchor, local, keep, send):
    xh, c = place[8], place[10]
    for side, out in ((1, send), (0, keep)):
        for dxh in range(2):
            rows = pl.ds(pl.multiple_of((c ^ side) * ROWS, ROWS), ROWS)
            at = xh ^ dxh
            for j in range(D // BLOCK):
                cols = pl.ds(j * BLOCK, BLOCK)
                a = anchor[at, 0, rows, cols].astype(jnp.float32)
                l = local[at, 0, rows, cols].astype(jnp.float32)
                out[0, dxh, :, cols] = code_and_decode(a - l)


def drift(place, anchor, local):
    block = pl.BlockSpec((2, 1, 2 * ROWS, D), lambda i, s: (0, (s[9] + i) % 4, 0, 0))
    out = pl.BlockSpec((1, 2, ROWS, D), lambda i, s: (i, 0, 0, 0))
    shape = jax.ShapeDtypeStruct((4, 2, ROWS, D), jnp.float32)
    return pl.pallas_call(
        drift_kernel,
        out_shape=(shape, shape),
        grid_spec=pltpu.PrefetchScalarGridSpec(
            num_scalar_prefetch=1, grid=(4,), in_specs=[block, block], out_specs=[out, out]
        ),
        compiler_params=pltpu.CompilerParams(vmem_limit_bytes=16 * MIB),
        cost_estimate=pl.CostEstimate(flops=20_000_000, bytes_accessed=9_500_000, transcendentals=0),
        name="drift",
    )(place, anchor.reshape(2, 4, 2 * ROWS, D), local.reshape(2, 4, 2 * ROWS, D))


def step_kernel(place, kept, came, anchor, momentum, new_momentum, new_rows):
    for j in range(D // BLOCK):
        cols = pl.ds(j * BLOCK, BLOCK)
        outer_grad = (kept[:, cols] + came[:, cols]) / 16.0
        moved = outer_beta * momentum[:, cols] + outer_grad
        new_momentum[:, cols] = moved
        step = code_and_decode(outer_grad + outer_beta * moved)
        new_rows[:, cols] = (anchor[0, :, cols].astype(jnp.float32) - outer_rate * step).astype(jnp.bfloat16)


def outer_step(place, kept, came, anchor, momentum):
    whole = pl.BlockSpec((ROWS, D), lambda i, s: (0, 0))
    return pl.pallas_call(
        step_kernel,
        out_shape=(jax.ShapeDtypeStruct((ROWS, D), jnp.float32), jax.ShapeDtypeStruct((ROWS, D), jnp.bfloat16)),
        grid_spec=pltpu.PrefetchScalarGridSpec(
            num_scalar_prefetch=1,
            grid=(1,),
            in_specs=[whole, whole, pl.BlockSpec((1, ROWS, D), lambda i, s: (s[11], 0, 0)), whole],
            out_specs=[whole, whole],
        ),
        compiler_params=pltpu.CompilerParams(vmem_limit_bytes=8 * MIB),
        cost_estimate=pl.CostEstimate(flops=2_000_000, bytes_accessed=1_000_000, transcendentals=0),
        name="outer_step",
    )(place, kept, came, anchor.reshape(16, ROWS, D), momentum)


def place_kernel(place, mine, other, out):
    xh, c = place[8], place[10]
    for side, source in ((0, mine), (1, other)):
        for dxh in range(2):
            rows = pl.ds(pl.multiple_of((c ^ side) * ROWS, ROWS), ROWS)
            out[xh ^ dxh, 0, rows, :] = source[0, dxh]


def place_rows(place, mine, other):
    source = pl.BlockSpec((1, 2, ROWS, D), lambda i, s: (i, 0, 0, 0))
    return pl.pallas_call(
        place_kernel,
        out_shape=jax.ShapeDtypeStruct((2, 4, 2 * ROWS, D), jnp.bfloat16),
        grid_spec=pltpu.PrefetchScalarGridSpec(
            num_scalar_prefetch=1,
            grid=(4,),
            in_specs=[source, source],
            out_specs=pl.BlockSpec((2, 1, 2 * ROWS, D), lambda i, s: (0, (s[9] + i) % 4, 0, 0)),
        ),
        compiler_params=pltpu.CompilerParams(vmem_limit_bytes=8 * MIB),
        cost_estimate=pl.CostEstimate(flops=0, bytes_accessed=3_200_000, transcendentals=0),
        name="place_rows",
    )(place, mine, other)


ROOT = 0.7978845608028654
CUBIC = 0.044715


def gelu_kernel(place, pre, hidden_t, slope):
    x = pre[0].astype(jnp.float32)
    square = x * x
    t = jnp.tanh(ROOT * (x + CUBIC * (square * x)))
    half = 0.5 * (1.0 + t)
    hidden_t[...] = (x * half).astype(jnp.bfloat16).T
    slope[0] = half + 0.5 * x * (1.0 - t * t) * (ROOT * (1.0 + (3.0 * CUBIC) * square))


def gelu(place, pre_act):
    return pl.pallas_call(
        gelu_kernel,
        out_shape=(
            jax.ShapeDtypeStruct((FF, 8 * CHUNK), jnp.bfloat16),
            jax.ShapeDtypeStruct((8, CHUNK, FF), jnp.float32),
        ),
        grid_spec=pltpu.PrefetchScalarGridSpec(
            num_scalar_prefetch=1,
            grid=(8,),
            in_specs=[pl.BlockSpec((1, CHUNK, FF), lambda i, s: (s[i], 0, 0))],
            out_specs=[
                pl.BlockSpec((FF, CHUNK), lambda i, s: (0, i)),
                pl.BlockSpec((1, CHUNK, FF), lambda i, s: (i, 0, 0)),
            ],
        ),
        compiler_params=pltpu.CompilerParams(vmem_limit_bytes=16 * MIB),
        cost_estimate=pl.CostEstimate(flops=30_000_000, bytes_accessed=12_600_000, transcendentals=1_572_864),
        name="gelu",
    )(place, pre_act.reshape(8, CHUNK, FF))


def gathered(refs):
    return jnp.concatenate([ref[...] for ref in refs], axis=0) if len(refs) > 1 else refs[0][...]


def backward_kernel(plan, place, *refs):
    n_grad, hidden, weight, base, begun, size = plan
    refs = list(refs)
    grads, refs = refs[:n_grad], refs[n_grad:]
    w, refs = refs[0], refs[1:]
    slopes, refs = refs[: len(hidden)], refs[len(hidden) :]
    hts, refs = refs[: len(weight)], refs[len(weight) :]
    if base:
        acc, refs = refs[0], refs[1:]
    if begun:
        refs = refs[1:]
    if weight:
        out, refs = refs[0], refs[1:]
    pre_grad, staged, sems = refs
    j, steps = pl.program_id(0), pl.num_programs(0)
    slot = j % 2

    def copies(step, slot):
        cols = pl.ds(pl.multiple_of(step * size, size), size)
        return [
            pltpu.make_async_copy(
                staged.at[slot, pl.ds(k * CHUNK, CHUNK)], pre_grad.at[place[p], :, cols], sems.at[slot, k]
            )
            for k, p in enumerate(hidden)
        ]

    @pl.when(j >= 2)
    def _():
        for copy in copies(j - 2, slot):
            copy.wait()

    rows = gathered(grads)
    first = rows[rows.shape[0] - len(hidden) * CHUNK :]
    back = lax.dot_general(first, w[...], (((1,), (1,)), ((), ())), preferred_element_type=jnp.float32)
    for k in range(len(hidden)):
        block = pl.ds(k * CHUNK, CHUNK)
        staged[slot, block] = (back[k * CHUNK : (k + 1) * CHUNK] * slopes[k][0]).astype(jnp.bfloat16)
    for copy in copies(j, slot):
        copy.start()
    if weight:
        left = jnp.concatenate([ref[...] for ref in hts], axis=1)
        total = jnp.dot(left, rows, preferred_element_type=jnp.float32)
        if base:
            total = total + acc[...].astype(jnp.float32)
        out[...] = total.astype(out.dtype)

    @pl.when(j == steps - 1)
    def _():
        for copy in copies(j - 1, 1 - slot) + copies(j, slot):
            copy.wait()


def backward(place, grads, w, slope, hidden_t, pre_grad, hidden, weight=(), base=None, out_dtype=jnp.bfloat16, size=256):
    steps = FF // size
    in_specs = [pl.BlockSpec(g.shape, lambda j, s: (0, 0)) for g in grads]
    in_specs.append(pl.BlockSpec((size, D), lambda j, s: (j, 0)))
    in_specs += [pl.BlockSpec((1, CHUNK, size), lambda j, s, p=p: (p, 0, j)) for p in hidden]
    in_specs += [pl.BlockSpec((size, CHUNK), lambda j, s, p=p: (j, p)) for p in weight]
    operands = list(grads) + [w] + [slope] * len(hidden) + [hidden_t] * len(weight)
    if base is not None:
        in_specs.append(pl.BlockSpec((size, D), lambda j, s: (j, 0)))
        operands.append(base)
    aliases = {}
    if pre_grad is not None:
        in_specs.append(pl.BlockSpec(memory_space=pl.ANY))
        operands.append(pre_grad)
        aliases = {len(operands): int(bool(weight))}
    out_specs, out_shape = [], []
    if weight:
        out_specs.append(pl.BlockSpec((size, D), lambda j, s: (j, 0)))
        out_shape.append(jax.ShapeDtypeStruct((FF, D), out_dtype))
    out_specs.append(pl.BlockSpec(memory_space=pl.ANY))
    out_shape.append(jax.ShapeDtypeStruct((8, CHUNK, FF), jnp.bfloat16))
    plan = (len(grads), tuple(hidden), tuple(weight), base is not None, pre_grad is not None, size)
    flops = 2 * FF * D * CHUNK * (len(hidden) + len(weight))

    def kernel(place, *refs):
        backward_kernel(plan, place, *refs)

    return pl.pallas_call(
        kernel,
        out_shape=tuple(out_shape),
        grid_spec=pltpu.PrefetchScalarGridSpec(
            num_scalar_prefetch=1,
            grid=(steps,),
            in_specs=in_specs,
            out_specs=out_specs,
            scratch_shapes=[
                pltpu.VMEM((2, len(hidden) * CHUNK, size), jnp.bfloat16),
                pltpu.SemaphoreType.DMA((2, len(hidden))),
            ],
        ),
        input_output_aliases=aliases,
        compiler_params=pltpu.CompilerParams(vmem_limit_bytes=40 * MIB),
        cost_estimate=pl.CostEstimate(
            flops=flops, bytes_accessed=FF * D * 2 * (1 + 2 * bool(weight)), transcendentals=0
        ),
        name="backward",
    )(place, *operands)


def shards(anchor, local_params, momentum, out_grad, pre_act, down_weight):
    anchor, local, momentum = anchor[0], local_params[0, 0], momentum[0]
    own, pre, w = out_grad[0], pre_act[0], down_weight[0]
    number = lax.axis_index("rep") * 8 + lax.axis_index("shard")
    place = lax.dynamic_index_in_dim(jnp.asarray(place_table()), number, keepdims=False)

    ym = shift(own, y=1)
    yp = shift(own, y=-1)
    x = shift(own, xl=1)

    keep, send = drift(place, anchor, local)
    halves = keep + shift(send, c=1)
    sums = halves[0] + shift(halves[1], z=1) + shift(halves[2], z=2) + shift(halves[3], z=3)
    came = shift(sums[1], xh=1)
    new_momentum, rows = outer_step(place, sums[0], came, anchor, momentum)

    hidden_t, slope = gelu(place, pre)

    xyp = shift(yp, xl=1)
    xym = shift(x, y=1)
    y2 = shift(yp, y=-1)
    partial, pre_grad = backward(
        place, [own, ym, yp, x], w, slope, hidden_t, None, hidden=(0, 1, 2, 3), weight=(0, 1, 2, 3)
    )
    a, b, _ = PARTS
    last = [
        shift(y2[:a], xl=1),
        shift(xym[a : a + b], y=1),
        shift(xyp[a + b :], y=-1),
    ]
    (pre_grad,) = backward(place, [xyp, xym, y2], w, slope, hidden_t, pre_grad, hidden=(4, 5, 6))
    weight_grad, pre_grad = backward(
        place,
        [xyp, xym, y2, *last],
        w,
        slope,
        hidden_t,
        pre_grad,
        hidden=(7,),
        weight=(4, 5, 6, 7),
        base=partial,
    )

    pair = jnp.stack([rows, shift(rows, xh=1)])
    mine = jnp.stack([pair, shift(pair, z=3), shift(pair, z=2), shift(pair, z=1)])
    new_anchor = place_rows(place, mine, shift(mine, c=1))
    return (
        new_anchor.reshape(1, 256, D),
        new_momentum[None],
        pre_grad.reshape(1, 8 * CHUNK, FF),
        weight_grad[None],
    )


def solution(mesh):
    return jax.shard_map(
        shards,
        mesh=mesh,
        in_specs=(
            P("shard", None, None),
            P("rep", "shard", None, None),
            P("shard", "rep", None),
            P("rep", "shard", None),
            P("rep", None, "shard"),
            P("rep", "shard", None),
        ),
        out_specs=(
            P("shard", None, None),
            P("shard", "rep", None),
            P("rep", None, "shard"),
            P("rep", "shard", None),
        ),
        check_vma=False,
    )
```

time: 311 us -> 106 us (0.34)
  waiting for transfers between devices: 223 us -> 17.7 us
  Pallas kernels: 0 us -> 52 us
  matrix products: 32.3 us -> 0 us
  starting transfers between devices: 0.12 us -> 31.3 us
  blocking collectives: 23.4 us -> 0 us
  between operations: 13.8 us -> 0.83 us
  other arithmetic: 11.8 us -> 0.45 us
    all_gather x2 -> x0, waiting for transfers between devices: 145 us -> none  [the longest x1 125 us: shards(): grad_rows = lax.all_gather(out_grad, 'shard', axis=1, tiled=True)[0]]
    reduce_scatter x1 -> x0, waiting for transfers between devices: 77.6 us -> none  [shards(): lax.psum_scatter(decode(drift_code, drift_scale), 'rep', scatter_dimensio...]
    pallas_call x0 -> x7, Pallas kernels: none -> 52 us  [the longest x3 40.5 us: backward(): pl.pallas_call(kernel, out_shape=tuple(out_shape), grid_spec=pltpu.Prefet...]
    dot_general x2 -> x0, matrix products: 32.3 us -> none  [the longest x1 16.7 us: shards(): lax.dot_general(grad_rows, weight, (((1,), (1,)), ((), ())), preferred_el...]
    ppermute x0 -> x19, starting transfers between devices: none -> 31.3 us  [shift(): return lax.ppermute(array, AXES, pairs)]
    all_gather x1 -> x0, blocking collectives: 23.4 us -> none  [shards(): lax.all_gather(step_scale, 'rep', axis=1, tiled=True)]
    ppermute x0 -> x19, waiting for transfers between devices: none -> 17.7 us  [shift(): return lax.ppermute(array, AXES, pairs)]
    convert_element_type x5 -> x0, other arithmetic: 5.79 us -> none  [the longest x1 4.65 us: shards(): (anchor.astype(jnp.float32) - outer_rate * decode(whole_code, whole_scale...]
  transfers between devices with their start and end apart: 3 -> 19, of which waited for: 3 -> 4; matrix products, arithmetic and copies ran while one was open for 2% -> 1% of each run, Pallas kernels for 0% -> 45%
where the time goes in v1:
time: 106 us
  Pallas kernels  52 us (49%)
  starting transfers between devices  31.3 us (30%)
  waiting for transfers between devices  17.7 us (17%)
  local copies, waits for them, and re-layouts  3.7 us (3%)
    pallas_call x3, Pallas kernels, backward(): pl.pallas_call(kernel, out_shape=tuple(out_shape), grid_spec=pltpu.Prefet...  40.5 us
    ppermute x19, starting transfers between devices, shift(): return lax.ppermute(array, AXES, pairs)  31.3 us
    ppermute x19, waiting for transfers between devices, shift(): return lax.ppermute(array, AXES, pairs)  17.7 us
    pallas_call x1, Pallas kernels, gelu(): pl.pallas_call(gelu_kernel, out_shape=(jax.ShapeDtypeStruct((FF, 8 * CHUN...  5.71 us
    unnamed x12, local copies, waits for them, and re-layouts  2.84 us
    pallas_call x1, Pallas kernels, drift(): pl.pallas_call(drift_kernel, out_shape=(shape, shape), grid_spec=pltpu.Pr...  2.29 us
    pallas_call x1, Pallas kernels, place_rows(): pl.pallas_call(place_kernel, out_shape=jax.ShapeDtypeStruct((2, 4, 2 * RO...  2.27 us
  transfers between devices with their start and end apart: 19, of which 4 were waited for; matrix products, arithmetic and copies ran while one was open for 1% of the time, Pallas kernels for 45%

profile of v1, /device:TPU:1, one launch (start us, length us, event | category | flops | bytes accessed | tf_op | source)
XLA Modules:
  0.0 106.0 jit_solution(8782079588564928797)
XLA Ops:
  0.6 0.7 dynamic-slice_bitcast_fusion.place
  1.3 1.4 %copy-done = bf16[1,256,3072]{2,1,0:T(8,128)(2,1)S(1)} copy-done((bf16[1,256,3072]{2,1,0:T(8,128)(2,1)S(1)}, bf16[1,256,3072]{2,1,0:T(8,128)(2,1)}, u32[]{:S(2)}) %copy-start) | copy-done | bytes 1572888
  2.7 1.4 %copy-done.3 = bf16[1,1,256,3072]{3,2,1,0:T(8,128)(2,1)S(1)} copy-done((bf16[1,1,256,3072]{3,2,1,0:T(8,128)(2,1)S(1)}, bf16[1,1,256,3072]{3,2,1,0:T(8,128)(2,1)}, u32[]{:S(2)}) %copy-start.3) | copy-done | bytes 1572888
  4.2 2.3 %drift.1 = (f32[4,2,16,3072]{3,2,1,0:T(8,128)S(1)}, f32[4,2,16,3072]{3,2,1,0:T(8,128)S(1)}) custom-call(s32[12]{0:T(128)S(1)} %dynamic-slice_bitcast_fusion.place, bf16[2,4,32,3072]{3,2,1,0:T(8,128)(2,1)S(1)} %bitcast.38, bf16[2,4,32,3072]{3,2,1,0:T(8,128)(2,1)S(1)} %bitcast.41), custom_call_target="tpu_custom_call" | custom-call | flops 20000000 | bytes 9500000 | tf_op jit(solution)/shard_map/drift/pallas_call | solution.py:73
  6.5 1.5 %collective-permute-start = (f32[4,2,16,3072]{3,2,1,0:T(8,128)S(1)}, f32[4,2,16,3072]{3,2,1,0:T(8,128)S(1)}, u32[]{:S(2)}, u32[]{:S(2)}) collective-permute-start(f32[4,2,16,3072]{3,2,1,0:T(8,128)S(1)} %get-tuple-element.15), channel_id=1, source_target_pairs={{0,8},{1,9},{2,10},{3,11},{4,12},{5,13},{6,14},{7,15},{8,0},{9,1},... | collective-permute-start | bytes 4718600 | tf_op jit(solution)/shard_map/ppermute | solution.py:39
  8.0 2.8 %collective-permute-start.10 = (bf16[128,3072]{1,0:T(8,128)(2,1)S(1)}, bf16[128,3072]{1,0:T(8,128)(2,1)S(1)}, u32[]{:S(2)}, u32[]{:S(2)}) collective-permute-start(bf16[128,3072]{1,0:T(8,128)(2,1)S(1)} %bitcast.42), channel_id=1, source_target_pairs={{0,6},{1,7},{2,0},{3,1},{4,2},{5,3},{6,4},{7,5},{8,14},{9,15},{10,... | collective-permute-start | bytes 2359304 | tf_op jit(solution)/shard_map/ppermute | solution.py:39
  10.8 0.2 collective-permute-done
  11.0 0.2 add.21
  11.2 0.0 copy-start.1
  11.2 0.0 copy-start.5
  11.3 0.0 copy-start.2
  11.3 0.1 slice_bitcast_fusion.2
  11.4 1.8 %collective-permute-start.1 = (f32[2,16,3072]{2,1,0:T(8,128)S(1)}, f32[2,16,3072]{2,1,0:T(8,128)S(1)}, u32[]{:S(2)}, u32[]{:S(2)}) collective-permute-start(f32[2,16,3072]{2,1,0:T(8,128)S(1)} %get-tuple-element.24), channel_id=1, source_target_pairs={{0,16},{1,17},{2,18},{3,19},{4,20},{5,21},{6,22},{7,23},{8,24},{9,... | collective-permute-start | bytes 1179656 | tf_op jit(solution)/shard_map/ppermute | solution.py:39
  13.1 3.3 %collective-permute-start.2 = (f32[2,16,3072]{2,1,0:T(8,128)S(1)}, f32[2,16,3072]{2,1,0:T(8,128)S(1)}, u32[]{:S(2)}, u32[]{:S(2)}) collective-permute-start(f32[2,16,3072]{2,1,0:T(8,128)S(1)} %get-tuple-element.26), channel_id=1, source_target_pairs={{0,32},{1,33},{2,34},{3,35},{4,36},{5,37},{6,38},{7,39},{8,40},{9,... | collective-permute-start | bytes 1179656 | tf_op jit(solution)/shard_map/ppermute | solution.py:39
  16.4 0.7 collective-permute-start.3
  17.2 1.2 %collective-permute-start.12 = (bf16[128,3072]{1,0:T(8,128)(2,1)S(1)}, bf16[128,3072]{1,0:T(8,128)(2,1)S(1)}, u32[]{:S(2)}, u32[]{:S(2)}) collective-permute-start(bf16[128,3072]{1,0:T(8,128)(2,1)S(1)} %bitcast.43), channel_id=1, source_target_pairs={{0,1},{1,0},{2,3},{3,2},{4,5},{5,4},{6,7},{7,6},{8,9},{9,8},{10,11... | collective-permute-start | bytes 2359304 | tf_op jit(solution)/shard_map/ppermute | solution.py:39
  18.4 9.3 %collective-permute-done.10.refs_2_ = bf16[128,3072]{1,0:T(8,128)(2,1)S(1)} collective-permute-done((bf16[128,3072]{1,0:T(8,128)(2,1)S(1)}, bf16[128,3072]{1,0:T(8,128)(2,1)S(1)}, u32[]{:S(2)}, u32[]{:S(2)}) %collective-permute-start.10) | collective-permute-done | bytes 786464 | tf_op jit(solution)/shard_map/ppermute | solution.py:39
  27.7 0.8 collective-permute-start.18
  28.4 0.0 collective-permute-done.1
  28.4 2.7 %collective-permute-start.14 = (bf16[128,3072]{1,0:T(8,128)(2,1)S(1)}, bf16[128,3072]{1,0:T(8,128)(2,1)S(1)}, u32[]{:S(2)}, u32[]{:S(2)}) collective-permute-start(bf16[128,3072]{1,0:T(8,128)(2,1)S(1)} %collective-permute-done.10.refs_2_), channel_id=1, source_target_pairs={{0,6},{1,7},{2,0},{3,1},{4,2},{5,3},{6,4},{7,5},{8,14},{9,15},{10,... | collective-permute-start | bytes 2359304 | tf_op jit(solution)/shard_map/ppermute | solution.py:39
  31.1 2.6 %collective-permute-done.2 = f32[2,16,3072]{2,1,0:T(8,128)S(1)} collective-permute-done((f32[2,16,3072]{2,1,0:T(8,128)S(1)}, f32[2,16,3072]{2,1,0:T(8,128)S(1)}, u32[]{:S(2)}, u32[]{:S(2)}) %collective-permute-start.2) | collective-permute-done | bytes 393248 | tf_op jit(solution)/shard_map/ppermute | solution.py:39
  33.7 0.0 collective-permute-done.3
  33.7 0.1 fusion.2
  33.9 2.8 %collective-permute-start.4 = (f32[16,3072]{1,0:T(8,128)S(1)}, f32[16,3072]{1,0:T(8,128)S(1)}, u32[]{:S(2)}, u32[]{:S(2)}) collective-permute-start(f32[16,3072]{1,0:T(8,128)S(1)} %get-tuple-element.27), channel_id=1, source_target_pairs={{0,64},{1,65},{2,66},{3,67},{4,68},{5,69},{6,70},{7,71},{8,72},{9,... | collective-permute-start | bytes 589832 | tf_op jit(solution)/shard_map/ppermute | solution.py:39
  36.7 5.5 %collective-permute-done.4.came = f32[16,3072]{1,0:T(8,128)S(1)} collective-permute-done((f32[16,3072]{1,0:T(8,128)S(1)}, f32[16,3072]{1,0:T(8,128)S(1)}, u32[]{:S(2)}, u32[]{:S(2)}) %collective-permute-start.4) | collective-permute-done | bytes 196640 | tf_op jit(solution)/shard_map/ppermute | solution.py:39
  42.2 1.3 %outer_step.1 = (f32[16,3072]{1,0:T(8,128)}, bf16[16,3072]{1,0:T(8,128)(2,1)S(1)}) custom-call(s32[12]{0:T(128)S(1)} %dynamic-slice_bitcast_fusion.place, f32[16,3072]{1,0:T(8,128)S(1)} %get-tuple-element.28.kept, f32[16,3072]{1,0:T(8,128)S(1)} %collective-permute-done.4.came, bf16[16,16,3072]{2,1,0:T(8,128)(2,1)S(1)} %bitcast.39, f32[16,3072]{1,0:T(8,128)S(1)} %bitcast.46), custom_call_target="tpu_custom_call" | custom-call | flops 2000000 | bytes 1000000 | tf_op jit(solution)/shard_map/outer_step/pallas_call | solution.py:97
  43.5 1.2 %collective-permute-start.5 = (bf16[16,3072]{1,0:T(8,128)(2,1)S(1)}, bf16[16,3072]{1,0:T(8,128)(2,1)S(1)}, u32[]{:S(2)}, u32[]{:S(2)}) collective-permute-start(bf16[16,3072]{1,0:T(8,128)(2,1)S(1)} %get-tuple-element.16), channel_id=1, source_target_pairs={{0,64},{1,65},{2,66},{3,67},{4,68},{5,69},{6,70},{7,71},{8,72},{9,... | collective-permute-start | bytes 294920 | tf_op jit(solution)/shard_map/ppermute | solution.py:39
  44.7 5.7 %gelu.1 = (bf16[1536,1024]{1,0:T(8,128)(2,1)S(1)}, f32[8,128,1536]{2,1,0:T(8,128)S(1)}) custom-call(s32[12]{0:T(128)S(1)} %dynamic-slice_bitcast_fusion.place, bf16[8,128,1536]{2,1,0:T(8,128)(2,1)S(1)} %bitcast.40), custom_call_target="tpu_custom_call" | custom-call | flops 30000000 | bytes 12600000 | tf_op jit(solution)/shard_map/gelu/pallas_call | solution.py:151
  50.4 0.4 collective-permute-start.11
  50.8 0.0 collective-permute-done.12.refs_3_
  50.8 1.3 %collective-permute-start.13 = (bf16[128,3072]{1,0:T(8,128)(2,1)S(1)}, bf16[128,3072]{1,0:T(8,128)(2,1)S(1)}, u32[]{:S(2)}, u32[]{:S(2)}) collective-permute-start(bf16[128,3072]{1,0:T(8,128)(2,1)S(1)} %collective-permute-done.12.refs_3_), channel_id=1, source_target_pairs={{0,2},{1,3},{2,4},{3,5},{4,6},{5,7},{6,0},{7,1},{8,10},{9,11},{10,... | collective-permute-start | bytes 2359304 | tf_op jit(solution)/shard_map/ppermute | solution.py:39
  52.1 0.0 collective-permute-done.5
  52.1 3.4 %collective-permute-start.6 = (bf16[2,16,3072]{2,1,0:T(8,128)(2,1)S(1)}, bf16[2,16,3072]{2,1,0:T(8,128)(2,1)S(1)}, u32[]{:S(2)}, u32[]{:S(2)}) collective-permute-start(bf16[2,16,3072]{2,1,0:T(8,128)(2,1)S(1)} %get-tuple-element.30), channel_id=1, source_target_pairs={{0,48},{1,49},{2,50},{3,51},{4,52},{5,53},{6,54},{7,55},{8,56},{9,... | collective-permute-start | bytes 589832 | tf_op jit(solution)/shard_map/ppermute | solution.py:39
  55.5 0.1 collective-permute-start.7
  55.6 0.6 collective-permute-start.8
  56.2 15.8 %backward.3 = (bf16[1536,3072]{1,0:T(8,128)(2,1)}, bf16[8,128,1536]{2,1,0:T(8,128)(2,1)}) custom-call(s32[12]{0:T(128)S(1)} %dynamic-slice_bitcast_fusion.place, bf16[128,3072]{1,0:T(8,128)(2,1)S(1)} %bitcast.45, bf16[128,3072]{1,0:T(8,128)(2,1)S(1)} %collective-permute-done.18.refs_1_, bf16[128,3072]{1,0:T(8,128)(2,1)S(1)} %collective-permute-done.10.refs_2_, ...), custom_call_target="tpu_custom_call" | custom-call | flops 9663676416 | bytes 28311552 | tf_op jit(solution)/shard_map/backward/pallas_call | solution.py:255
  72.1 0.0 collective-permute-done.11.refs_0_
  72.1 1.2 %collective-permute-start.15 = (bf16[48,3072]{1,0:T(8,128)(2,1)S(1)}, bf16[48,3072]{1,0:T(8,128)(2,1)S(1)}, u32[]{:S(2)}, u32[]{:S(2)}) collective-permute-start(bf16[48,3072]{1,0:T(8,128)(2,1)S(1)} %slice.42), channel_id=1, source_target_pairs={{0,1},{1,0},{2,3},{3,2},{4,5},{5,4},{6,7},{7,6},{8,9},{9,8},{10,11... | collective-permute-start | bytes 884744 | tf_op jit(solution)/shard_map/ppermute | solution.py:39
  73.4 0.0 collective-permute-done.13.refs_1_
  73.4 1.5 %collective-permute-start.17 = (bf16[32,3072]{1,0:T(8,128)(2,1)S(1)}, bf16[32,3072]{1,0:T(8,128)(2,1)S(1)}, u32[]{:S(2)}, u32[]{:S(2)}) collective-permute-start(bf16[32,3072]{1,0:T(8,128)(2,1)S(1)} %slice.44), channel_id=1, source_target_pairs={{0,6},{1,7},{2,0},{3,1},{4,2},{5,3},{6,4},{7,5},{8,14},{9,15},{10,... | collective-permute-start | bytes 589832 | tf_op jit(solution)/shard_map/ppermute | solution.py:39
  74.9 0.0 collective-permute-done.6
  74.9 0.1 collective-permute-start.16
  75.0 0.0 collective-permute-done.8
  75.0 0.1 pad_maximum_fusion.mine
  75.1 3.9 %collective-permute-start.9 = (bf16[4,2,16,3072]{3,2,1,0:T(8,128)(2,1)S(1)}, bf16[4,2,16,3072]{3,2,1,0:T(8,128)(2,1)S(1)}, u32[]{:S(2)}, u32[]{:S(2)}) collective-permute-start(bf16[4,2,16,3072]{3,2,1,0:T(8,128)(2,1)S(1)} %pad_maximum_fusion.mine), channel_id=1, source_target_pairs={{0,8},{1,9},{2,10},{3,11},{4,12},{5,13},{6,14},{7,15},{8,0},{9,1},... | collective-permute-start | bytes 2359304 | tf_op jit(solution)/shard_map/ppermute | solution.py:39
  79.0 9.2 %backward.4.refs_13_ = bf16[8,128,1536]{2,1,0:T(8,128)(2,1)} custom-call(s32[12]{0:T(128)S(1)} %dynamic-slice_bitcast_fusion.place, bf16[128,3072]{1,0:T(8,128)(2,1)S(1)} %collective-permute-done.11.refs_0_, bf16[128,3072]{1,0:T(8,128)(2,1)S(1)} %collective-permute-done.13.refs_1_, ...), custom_call_target="tpu_custom_call", output_to_operand_aliasing={{}: (8, {})} | custom-call | flops 3623878656 | bytes 9437184 | tf_op jit(solution)/shard_map/backward/pallas_call | solution.py:255
  88.3 15.4 %backward.5 = (bf16[1536,3072]{1,0:T(8,128)(2,1)}, bf16[8,128,1536]{2,1,0:T(8,128)(2,1)}) custom-call(s32[12]{0:T(128)S(1)} %dynamic-slice_bitcast_fusion.place, bf16[128,3072]{1,0:T(8,128)(2,1)S(1)} %collective-permute-done.11.refs_0_, bf16[128,3072]{1,0:T(8,128)(2,1)S(1)} %collective-permute-done.13.refs_1_, ...), custom_call_target="tpu_custom_call", output_to_operand_aliasing={{1}: (14, {})} | custom-call | flops 6039797760 | bytes 28311552 | tf_op jit(solution)/shard_map/backward/pallas_call | solution.py:255
  103.7 2.3 %place_rows.1 = bf16[2,4,32,3072]{3,2,1,0:T(8,128)(2,1)} custom-call(s32[12]{0:T(128)S(1)} %dynamic-slice_bitcast_fusion.place, bf16[4,2,16,3072]{3,2,1,0:T(8,128)(2,1)S(1)} %pad_maximum_fusion.mine, bf16[4,2,16,3072]{3,2,1,0:T(8,128)(2,1)S(1)} %collective-permute-done.9.other), custom_call_target="tpu_custom_call" | custom-call | bytes 3200000 | tf_op jit(solution)/shard_map/place_rows/pallas_call | solution.py:122
  (19 shorter events, 0.1 us)
Async XLA Ops:
  1.3 1.4 %copy-start = (bf16[1,256,3072]{2,1,0:T(8,128)(2,1)S(1)}, bf16[1,256,3072]{2,1,0:T(8,128)(2,1)}, u32[]{:S(2)}) copy-start(bf16[1,256,3072]{2,1,0:T(8,128)(2,1)} %param.7) | copy-start | bytes 4718596
  2.7 1.4 %copy-start.3 = (bf16[1,1,256,3072]{3,2,1,0:T(8,128)(2,1)S(1)}, bf16[1,1,256,3072]{3,2,1,0:T(8,128)(2,1)}, u32[]{:S(2)}) copy-start(bf16[1,1,256,3072]{3,2,1,0:T(8,128)(2,1)} %param.8) | copy-start | bytes 4718596
  4.2 3.8 %copy-start.4 = (bf16[1,128,3072]{2,1,0:T(8,128)(2,1)S(1)}, bf16[1,128,3072]{2,1,0:T(8,128)(2,1)}, u32[]{:S(2)}) copy-start(bf16[1,128,3072]{2,1,0:T(8,128)(2,1)} %param.10) | copy-start | bytes 2359300
  6.5 4.5 %collective-permute-start = (f32[4,2,16,3072]{3,2,1,0:T(8,128)S(1)}, f32[4,2,16,3072]{3,2,1,0:T(8,128)S(1)}, u32[]{:S(2)}, u32[]{:S(2)}) collective-permute-start(f32[4,2,16,3072]{3,2,1,0:T(8,128)S(1)} %get-tuple-element.15), channel_id=1, source_target_pairs={{0,8},{1,9},{2,10},{3,11},{4,12},{5,13},{6,14},{7,15},{8,0},{9,1},... | collective-permute-start | bytes 4718600 | tf_op jit(solution)/shard_map/ppermute | solution.py:39
  8.0 19.7 %collective-permute-start.10 = (bf16[128,3072]{1,0:T(8,128)(2,1)S(1)}, bf16[128,3072]{1,0:T(8,128)(2,1)S(1)}, u32[]{:S(2)}, u32[]{:S(2)}) collective-permute-start(bf16[128,3072]{1,0:T(8,128)(2,1)S(1)} %bitcast.42), channel_id=1, source_target_pairs={{0,6},{1,7},{2,0},{3,1},{4,2},{5,3},{6,4},{7,5},{8,14},{9,15},{10,... | collective-permute-start | bytes 2359304 | tf_op jit(solution)/shard_map/ppermute | solution.py:39
  11.2 31.0 %copy-start.1 = (bf16[1,256,3072]{2,1,0:T(8,128)(2,1)S(1)}, bf16[1,256,3072]{2,1,0:T(8,128)(2,1)}, u32[]{:S(2)}) copy-start(bf16[1,256,3072]{2,1,0:T(8,128)(2,1)} %param.7) | copy-start | bytes 4718596
  11.2 31.0 %copy-start.5 = (f32[1,16,3072]{2,1,0:T(8,128)S(1)}, f32[1,16,3072]{2,1,0:T(8,128)}, u32[]{:S(2)}) copy-start(f32[1,16,3072]{2,1,0:T(8,128)} %param.9) | copy-start | bytes 589828
  11.3 33.4 %copy-start.2 = (bf16[1,1024,1536]{2,1,0:T(8,128)(2,1)S(1)}, bf16[1,1024,1536]{2,1,0:T(8,128)(2,1)}, u32[]{:S(2)}) copy-start(bf16[1,1024,1536]{2,1,0:T(8,128)(2,1)} %param.11) | copy-start | bytes 9437188
  11.4 17.1 %collective-permute-start.1 = (f32[2,16,3072]{2,1,0:T(8,128)S(1)}, f32[2,16,3072]{2,1,0:T(8,128)S(1)}, u32[]{:S(2)}, u32[]{:S(2)}) collective-permute-start(f32[2,16,3072]{2,1,0:T(8,128)S(1)} %get-tuple-element.24), channel_id=1, source_target_pairs={{0,16},{1,17},{2,18},{3,19},{4,20},{5,21},{6,22},{7,23},{8,24},{9,... | collective-permute-start | bytes 1179656 | tf_op jit(solution)/shard_map/ppermute | solution.py:39
  13.1 20.6 %collective-permute-start.2 = (f32[2,16,3072]{2,1,0:T(8,128)S(1)}, f32[2,16,3072]{2,1,0:T(8,128)S(1)}, u32[]{:S(2)}, u32[]{:S(2)}) collective-permute-start(f32[2,16,3072]{2,1,0:T(8,128)S(1)} %get-tuple-element.26), channel_id=1, source_target_pairs={{0,32},{1,33},{2,34},{3,35},{4,36},{5,37},{6,38},{7,39},{8,40},{9,... | collective-permute-start | bytes 1179656 | tf_op jit(solution)/shard_map/ppermute | solution.py:39
  16.4 17.3 %collective-permute-start.3 = (f32[2,16,3072]{2,1,0:T(8,128)S(1)}, f32[2,16,3072]{2,1,0:T(8,128)S(1)}, u32[]{:S(2)}, u32[]{:S(2)}) collective-permute-start(f32[2,16,3072]{2,1,0:T(8,128)S(1)} %get-tuple-element.25), channel_id=1, source_target_pairs={{0,48},{1,49},{2,50},{3,51},{4,52},{5,53},{6,54},{7,55},{8,56},{9,... | collective-permute-start | bytes 1179656 | tf_op jit(solution)/shard_map/ppermute | solution.py:39
  17.2 33.6 %collective-permute-start.12 = (bf16[128,3072]{1,0:T(8,128)(2,1)S(1)}, bf16[128,3072]{1,0:T(8,128)(2,1)S(1)}, u32[]{:S(2)}, u32[]{:S(2)}) collective-permute-start(bf16[128,3072]{1,0:T(8,128)(2,1)S(1)} %bitcast.43), channel_id=1, source_target_pairs={{0,1},{1,0},{2,3},{3,2},{4,5},{5,4},{6,7},{7,6},{8,9},{9,8},{10,11... | collective-permute-start | bytes 2359304 | tf_op jit(solution)/shard_map/ppermute | solution.py:39
  27.7 27.9 %collective-permute-start.18 = (bf16[128,3072]{1,0:T(8,128)(2,1)S(1)}, bf16[128,3072]{1,0:T(8,128)(2,1)S(1)}, u32[]{:S(2)}, u32[]{:S(2)}) collective-permute-start(bf16[128,3072]{1,0:T(8,128)(2,1)S(1)} %bitcast.44), channel_id=1, source_target_pairs={{0,2},{1,3},{2,4},{3,5},{4,6},{5,7},{6,0},{7,1},{8,10},{9,11},{10,... | collective-permute-start | bytes 2359304 | tf_op jit(solution)/shard_map/ppermute | solution.py:39
  28.4 27.2 %collective-permute-start.14 = (bf16[128,3072]{1,0:T(8,128)(2,1)S(1)}, bf16[128,3072]{1,0:T(8,128)(2,1)S(1)}, u32[]{:S(2)}, u32[]{:S(2)}) collective-permute-start(bf16[128,3072]{1,0:T(8,128)(2,1)S(1)} %collective-permute-done.10.refs_2_), channel_id=1, source_target_pairs={{0,6},{1,7},{2,0},{3,1},{4,2},{5,3},{6,4},{7,5},{8,14},{9,15},{10,... | collective-permute-start | bytes 2359304 | tf_op jit(solution)/shard_map/ppermute | solution.py:39
  33.9 8.3 %collective-permute-start.4 = (f32[16,3072]{1,0:T(8,128)S(1)}, f32[16,3072]{1,0:T(8,128)S(1)}, u32[]{:S(2)}, u32[]{:S(2)}) collective-permute-start(f32[16,3072]{1,0:T(8,128)S(1)} %get-tuple-element.27), channel_id=1, source_target_pairs={{0,64},{1,65},{2,66},{3,67},{4,68},{5,69},{6,70},{7,71},{8,72},{9,... | collective-permute-start | bytes 589832 | tf_op jit(solution)/shard_map/ppermute | solution.py:39
  43.5 8.6 %collective-permute-start.5 = (bf16[16,3072]{1,0:T(8,128)(2,1)S(1)}, bf16[16,3072]{1,0:T(8,128)(2,1)S(1)}, u32[]{:S(2)}, u32[]{:S(2)}) collective-permute-start(bf16[16,3072]{1,0:T(8,128)(2,1)S(1)} %get-tuple-element.16), channel_id=1, source_target_pairs={{0,64},{1,65},{2,66},{3,67},{4,68},{5,69},{6,70},{7,71},{8,72},{9,... | collective-permute-start | bytes 294920 | tf_op jit(solution)/shard_map/ppermute | solution.py:39
  50.4 21.7 %collective-permute-start.11 = (bf16[128,3072]{1,0:T(8,128)(2,1)S(1)}, bf16[128,3072]{1,0:T(8,128)(2,1)S(1)}, u32[]{:S(2)}, u32[]{:S(2)}) collective-permute-start(bf16[128,3072]{1,0:T(8,128)(2,1)S(1)} %collective-permute-done.10.refs_2_), channel_id=1, source_target_pairs={{0,1},{1,0},{2,3},{3,2},{4,5},{5,4},{6,7},{7,6},{8,9},{9,8},{10,11... | collective-permute-start | bytes 2359304 | tf_op jit(solution)/shard_map/ppermute | solution.py:39
  50.8 22.6 %collective-permute-start.13 = (bf16[128,3072]{1,0:T(8,128)(2,1)S(1)}, bf16[128,3072]{1,0:T(8,128)(2,1)S(1)}, u32[]{:S(2)}, u32[]{:S(2)}) collective-permute-start(bf16[128,3072]{1,0:T(8,128)(2,1)S(1)} %collective-permute-done.12.refs_3_), channel_id=1, source_target_pairs={{0,2},{1,3},{2,4},{3,5},{4,6},{5,7},{6,0},{7,1},{8,10},{9,11},{10,... | collective-permute-start | bytes 2359304 | tf_op jit(solution)/shard_map/ppermute | solution.py:39
  52.1 22.8 %collective-permute-start.6 = (bf16[2,16,3072]{2,1,0:T(8,128)(2,1)S(1)}, bf16[2,16,3072]{2,1,0:T(8,128)(2,1)S(1)}, u32[]{:S(2)}, u32[]{:S(2)}) collective-permute-start(bf16[2,16,3072]{2,1,0:T(8,128)(2,1)S(1)} %get-tuple-element.30), channel_id=1, source_target_pairs={{0,48},{1,49},{2,50},{3,51},{4,52},{5,53},{6,54},{7,55},{8,56},{9,... | collective-permute-start | bytes 589832 | tf_op jit(solution)/shard_map/ppermute | solution.py:39
  55.5 19.5 %collective-permute-start.7 = (bf16[2,16,3072]{2,1,0:T(8,128)(2,1)S(1)}, bf16[2,16,3072]{2,1,0:T(8,128)(2,1)S(1)}, u32[]{:S(2)}, u32[]{:S(2)}) collective-permute-start(bf16[2,16,3072]{2,1,0:T(8,128)(2,1)S(1)} %get-tuple-element.30), channel_id=1, source_target_pairs={{0,32},{1,33},{2,34},{3,35},{4,36},{5,37},{6,38},{7,39},{8,40},{9,... | collective-permute-start | bytes 589832 | tf_op jit(solution)/shard_map/ppermute | solution.py:39
  55.6 19.4 %collective-permute-start.8 = (bf16[2,16,3072]{2,1,0:T(8,128)(2,1)S(1)}, bf16[2,16,3072]{2,1,0:T(8,128)(2,1)S(1)}, u32[]{:S(2)}, u32[]{:S(2)}) collective-permute-start(bf16[2,16,3072]{2,1,0:T(8,128)(2,1)S(1)} %get-tuple-element.30), channel_id=1, source_target_pairs={{0,16},{1,17},{2,18},{3,19},{4,20},{5,21},{6,22},{7,23},{8,24},{9,... | collective-permute-start | bytes 589832 | tf_op jit(solution)/shard_map/ppermute | solution.py:39
  72.1 16.1 %collective-permute-start.15 = (bf16[48,3072]{1,0:T(8,128)(2,1)S(1)}, bf16[48,3072]{1,0:T(8,128)(2,1)S(1)}, u32[]{:S(2)}, u32[]{:S(2)}) collective-permute-start(bf16[48,3072]{1,0:T(8,128)(2,1)S(1)} %slice.42), channel_id=1, source_target_pairs={{0,1},{1,0},{2,3},{3,2},{4,5},{5,4},{6,7},{7,6},{8,9},{9,8},{10,11... | collective-permute-start | bytes 884744 | tf_op jit(solution)/shard_map/ppermute | solution.py:39
  73.4 14.9 %collective-permute-start.17 = (bf16[32,3072]{1,0:T(8,128)(2,1)S(1)}, bf16[32,3072]{1,0:T(8,128)(2,1)S(1)}, u32[]{:S(2)}, u32[]{:S(2)}) collective-permute-start(bf16[32,3072]{1,0:T(8,128)(2,1)S(1)} %slice.44), channel_id=1, source_target_pairs={{0,6},{1,7},{2,0},{3,1},{4,2},{5,3},{6,4},{7,5},{8,14},{9,15},{10,... | collective-permute-start | bytes 589832 | tf_op jit(solution)/shard_map/ppermute | solution.py:39
  74.9 13.3 %collective-permute-start.16 = (bf16[48,3072]{1,0:T(8,128)(2,1)S(1)}, bf16[48,3072]{1,0:T(8,128)(2,1)S(1)}, u32[]{:S(2)}, u32[]{:S(2)}) collective-permute-start(bf16[48,3072]{1,0:T(8,128)(2,1)S(1)} %slice.43), channel_id=1, source_target_pairs={{0,2},{1,3},{2,4},{3,5},{4,6},{5,7},{6,0},{7,1},{8,10},{9,11},{10,... | collective-permute-start | bytes 884744 | tf_op jit(solution)/shard_map/ppermute | solution.py:39
  75.1 28.6 %collective-permute-start.9 = (bf16[4,2,16,3072]{3,2,1,0:T(8,128)(2,1)S(1)}, bf16[4,2,16,3072]{3,2,1,0:T(8,128)(2,1)S(1)}, u32[]{:S(2)}, u32[]{:S(2)}) collective-permute-start(bf16[4,2,16,3072]{3,2,1,0:T(8,128)(2,1)S(1)} %pad_maximum_fusion.mine), channel_id=1, source_target_pairs={{0,8},{1,9},{2,10},{3,11},{4,12},{5,13},{6,14},{7,15},{8,0},{9,1},... | collective-permute-start | bytes 2359304 | tf_op jit(solution)/shard_map/ppermute | solution.py:39

commit v2 on v0

v2 whole, which is shorter than its diff:
```python
import itertools

import jax
import jax.numpy as jnp
import numpy as np
from jax import lax
from jax.experimental import pallas as pl
from jax.experimental.pallas import tpu as pltpu
from jax.sharding import PartitionSpec as P

BLOCK = 128
D = 3072
FF = 1536
CHUNK = 128
ROWS = 16

epsilon = 1e-06
outer_beta = 0.9
outer_rate = 0.7

AXES = ("rep", "shard")
MIB = 1024 * 1024
PER_US = 1_000_000_000
VMEM = pl.BlockSpec(memory_space=pltpu.VMEM)
SMEM = pl.BlockSpec(memory_space=pltpu.SMEM)
HBM = pl.BlockSpec(memory_space=pltpu.HBM)
ANY = pl.BlockSpec(memory_space=pl.ANY)


def device_index(xh, z, c, y, xl):
    return ((xh % 2 * 4 + z % 4) * 2 + c % 2) * 8 + y % 4 * 2 + xl % 2


def every_device():
    return itertools.product(range(2), range(4), range(2), range(4), range(2))


def shift(array, xh=0, z=0, c=0, y=0, xl=0):
    pairs = []
    for at in every_device():
        step = y(at[2]) if callable(y) else y
        pairs.append((device_index(*at), device_index(at[0] + xh, at[1] + z, at[2] + c, at[3] + step, at[4] + xl)))
    return lax.ppermute(array, AXES, pairs)


def place_table():
    table = np.zeros((128, 12), np.int32)
    for at in every_device():
        xh, z, c, y, xl = at
        order = [(y, xl), (y - 1, xl), (y + 1, xl), (y, 1 - xl), (y + 1, 1 - xl), (y - 1, 1 - xl), (y + 2, xl), (y + 2, 1 - xl)]
        table[device_index(*at)] = [a % 4 * 2 + b for a, b in order] + [xh, z, c, (xh * 4 + z) * 2 + c]
    return table


def code_and_decode(values):
    scale = (jnp.max(jnp.abs(values), axis=-1, keepdims=True) + epsilon).astype(jnp.bfloat16).astype(jnp.float32)
    return (values / scale).astype(jnp.bfloat16).astype(jnp.float32) * scale


def call(kernel, place, operands, in_specs, out_shape, out_specs, scratch=(), limit=2, aliases=None, after=(), us=1.0):
    operands = [pltpu.with_memory_space_constraint(x, spec.memory_space) for x, spec in zip(operands, in_specs)]
    count, more = len(operands), len(after)
    after_specs = [HBM if x.size >= 8 * CHUNK * FF else ANY for x in after]
    after = [x if spec is ANY else pltpu.with_memory_space_constraint(x, pltpu.HBM) for x, spec in zip(after, after_specs)]

    def body(place, *refs):
        kernel(place, *refs[:count], *refs[count + more :])

    return pl.pallas_call(
        body,
        out_shape=out_shape,
        in_specs=[SMEM, *in_specs, *after_specs],
        out_specs=out_specs,
        scratch_shapes=list(scratch),
        input_output_aliases=aliases or {},
        compiler_params=pltpu.CompilerParams(vmem_limit_bytes=limit * MIB),
        cost_estimate=pl.CostEstimate(flops=int(us * PER_US), bytes_accessed=0, transcendentals=0),
        name=kernel.__name__,
    )(place, *operands, *after)


def drift_sums(place, anchor, own, other, kept, to_1, to_2, to_3, held, sems):
    xh, z, c = place[8], place[9], place[10]
    rows = pl.ds(pl.multiple_of(c * ROWS, ROWS), ROWS)
    copies = [
        [
            pltpu.make_async_copy(source.at[xh ^ dxh, (z + dz) % 4, rows], held.at[k, dz, dxh], sems.at[dz, k, dxh])
            for k, source in enumerate((anchor, own, other))
            for dxh in range(2)
        ]
        for dz in range(4)
    ]
    for copy in sum(copies, []):
        copy.start()
    for dz, out in enumerate((kept, to_1, to_2, to_3)):
        for copy in copies[dz]:
            copy.wait()

        @pl.loop(0, 2)
        def _(dxh):
            for j in range(D // BLOCK):
                cols = pl.ds(j * BLOCK, BLOCK)
                a = held[0, dz, dxh, :, cols].astype(jnp.float32)
                first = code_and_decode(a - held[1, dz, dxh, :, cols].astype(jnp.float32))
                second = code_and_decode(a - held[2, dz, dxh, :, cols].astype(jnp.float32))
                out[dxh, :, cols] = (first + second).astype(out.dtype)


def z_sums(place, kept, from_1, from_2, from_3, mine, send):
    for dxh, out in enumerate((mine, send)):
        total = kept[dxh] + from_1[dxh].astype(jnp.float32)
        total = total + from_2[dxh].astype(jnp.float32)
        out[...] = total + from_3[dxh].astype(jnp.float32)


def outer_step(place, kept, came, anchor, momentum, new_momentum, new_rows):
    rep = place[11]
    for j in range(D // BLOCK):
        cols = pl.ds(j * BLOCK, BLOCK)
        outer_grad = (kept[:, cols] + came[:, cols]) / 16.0
        moved = outer_beta * momentum[:, cols] + outer_grad
        new_momentum[:, cols] = moved
        step = code_and_decode(outer_grad + outer_beta * moved)
        new_rows[:, cols] = (anchor[rep, :, cols].astype(jnp.float32) - outer_rate * step).astype(jnp.bfloat16)


def pick(place, first, second, out):
    @pl.when(place[10] == 0)
    def _():
        out[...] = first[...]

    @pl.when(place[10] == 1)
    def _():
        out[...] = second[...]


def relay(place, *refs):
    pass


def stack(place, *refs):
    for k, ref in enumerate(refs[:-1]):
        refs[-1][k] = ref[...]


def place_rows(place, mine, other, out, sem):
    xh, z, c = place[8], place[9], place[10]
    copies = [
        pltpu.make_async_copy(
            rows.at[dz, dxh],
            out.at[xh ^ dxh, (z + dz) % 4, pl.ds(pl.multiple_of((c ^ side) * ROWS, ROWS), ROWS)],
            sem.at[8 * side + 2 * dz + dxh],
        )
        for side, rows in enumerate((mine, other))
        for dz in range(4)
        for dxh in range(2)
    ]
    for copy in copies:
        copy.start()
    for copy in copies:
        copy.wait()


ROOT = 0.7978845608028654
CUBIC = 0.044715
WIDTH = 256


def gelu(first):
    def kernel(place, pre, hidden_t, slope, held, sems):
        copies = [pltpu.make_async_copy(pre.at[place[first + i]], held.at[i], sems.at[i]) for i in range(4)]
        for copy in copies:
            copy.start()
        for i, copy in enumerate(copies):
            copy.wait()
            here = slice(i * CHUNK, (i + 1) * CHUNK)
            for j in range(FF // WIDTH):
                cols = slice(j * WIDTH, (j + 1) * WIDTH)
                x = held[i, :, cols].astype(jnp.float32)
                square = x * x
                t = jnp.tanh(ROOT * (x + CUBIC * (square * x)))
                half = 0.5 * (1.0 + t)
                hidden_t[cols, here] = (x * half).astype(jnp.bfloat16).T
                slope[here, cols] = half + 0.5 * x * (1.0 - t * t) * (ROOT * (1.0 + (3.0 * CUBIC) * square))

    kernel.__name__ = f"gelu_{first}"
    return kernel


def pre_grads(place, rows, w, slope, staged, pre_grad, sems, first):
    copies = []
    for j in range(FF // WIDTH):
        cols = slice(j * WIDTH, (j + 1) * WIDTH)
        if rows.shape[0] > CHUNK:
            back = lax.dot_general(rows[...], w[cols], (((1,), (1,)), ((), ())), preferred_element_type=jnp.float32)
        else:
            back = lax.dot_general(w[cols], rows[...], (((1,), (1,)), ((), ())), preferred_element_type=jnp.float32).T
        staged[:, cols] = (back * slope[:, cols]).astype(jnp.bfloat16)
        if j % 2:
            cols = pl.ds((j - 1) * WIDTH, 2 * WIDTH)
            for k in range(rows.shape[0] // CHUNK):
                source = staged.at[pl.ds(k * CHUNK, CHUNK), cols]
                copy = pltpu.make_async_copy(source, pre_grad.at[place[first + k], :, cols], sems.at[j // 2, k])
                copy.start()
                copies.append(copy)
    return copies


def join(chunks, rows):
    at = 0
    for chunk in chunks:
        rows[at : at + chunk.shape[0]] = chunk[...]
        at += chunk.shape[0]


def hidden_grad(first, count, again):
    def kernel(place, *refs):
        chunks, (w, slope) = refs[:count], refs[count : count + 2]
        pre_grad, staged, sems = refs[-3:]
        rows = chunks[0]
        if count > 1:
            rows = refs[-4 - again]
            join(chunks, rows)
        if again:
            refs[-4][...] = chunks[-1][...]
        at = first % 4 * CHUNK
        for copy in pre_grads(place, rows, w, slope.at[at : at + count * CHUNK], staged, pre_grad, sems, first):
            copy.wait()

    kernel.__name__ = f"hidden_grad_{first}"
    return kernel


def run_hidden_grad(place, first, chunks, w, slope, pre_grad=None, again=False, after=()):
    count = len(chunks)
    operands, specs = [*chunks, w, slope], [VMEM] * (count + 2)
    out_shape = [pltpu.VMEM((count * CHUNK, D), jnp.bfloat16)] * (count > 1) + [pltpu.VMEM((CHUNK, D), jnp.bfloat16)] * again
    aliases = {}
    if pre_grad is not None:
        operands, specs = operands + [pre_grad], specs + [HBM]
        aliases = {len(operands): len(out_shape)}
    return call(
        hidden_grad(first, count, again),
        place,
        operands,
        specs,
        (*out_shape, pltpu.HBM((8, CHUNK, FF), jnp.bfloat16)),
        (*[VMEM] * len(out_shape), HBM),
        [pltpu.VMEM((count * CHUNK, FF), jnp.bfloat16), pltpu.SemaphoreType.DMA((FF // WIDTH // 2, count))],
        limit=8,
        aliases=aliases,
        after=after,
        us=1.5 + 1.3 * count,
    )


WIDE = 512


def weight_grad_first(place, rows, hidden_t, partial, token):
    token[...] = jnp.zeros_like(token)
    for j in range(D // WIDE):
        cols = slice(j * WIDE, (j + 1) * WIDE)
        partial[:, cols] = jnp.dot(hidden_t[...], rows[:, cols], preferred_element_type=jnp.float32).astype(jnp.bfloat16)


TALL = 512


def weight_grad_last(place, most, chunk, hidden_t, partial, weight_grad, rows, block, sems):
    join((most, chunk), rows)
    stored = []
    for i in range(FF // TALL):
        here = slice(i * TALL, (i + 1) * TALL)
        if i >= 2:
            stored[i - 2].wait()
        for j in range(D // WIDE):
            cols = slice(j * WIDE, (j + 1) * WIDE)
            total = jnp.dot(hidden_t[here], rows[:, cols], preferred_element_type=jnp.float32)
            block[i % 2, :, cols] = (partial[here, cols].astype(jnp.float32) + total).astype(jnp.bfloat16)
        store = pltpu.make_async_copy(block.at[i % 2], weight_grad.at[here], sems.at[i % 2])
        store.start()
        stored.append(store)
    for store in stored[-2:]:
        store.wait()


def shards(anchor, local_params, momentum, out_grad, pre_act, down_weight):
    anchor, local, momentum = anchor[0], local_params[0, 0], momentum[0]
    own, pre, w = out_grad[0], pre_act[0], down_weight[0]
    number = lax.axis_index("rep") * 8 + lax.axis_index("shard")
    place = lax.dynamic_index_in_dim(jnp.asarray(place_table()), number, keepdims=False)
    f32, bf16 = jnp.float32, jnp.bfloat16

    ym = shift(own, y=1)
    yp = shift(own, y=-1)
    x = shift(own, xl=1)

    view = (2, 4, 2 * ROWS, D)
    local = local.reshape(view)
    pair = pltpu.VMEM((2, ROWS, D), bf16)
    ht_0, slope_0 = call(
        gelu(0),
        place,
        [pre.reshape(8, CHUNK, FF)],
        [HBM],
        (pltpu.VMEM((FF, 4 * CHUNK), bf16), pltpu.VMEM((4 * CHUNK, FF), f32)),
        (VMEM,) * 2,
        [pltpu.VMEM((4, CHUNK, FF), bf16), pltpu.SemaphoreType.DMA((4,))],
        limit=6,
        us=2.8,
        after=(),
    )
    kept, to_1, to_2, to_3 = call(
        drift_sums,
        place,
        [anchor.reshape(view), local, shift(local, c=1)],
        [HBM] * 3,
        (pltpu.VMEM((2, ROWS, D), f32), pair, pair, pair),
        (VMEM,) * 4,
        [pltpu.VMEM((3, 4, 2, ROWS, D), bf16), pltpu.SemaphoreType.DMA((4, 3, 2))],
        limit=4,
        us=3.0,
        after=[slope_0],
    )
    from_z = [shift(to_1, z=1), shift(to_2, z=2), shift(to_3, z=3)]
    mine, send = call(
        z_sums,
        place,
        [kept, *from_z],
        [VMEM] * 4,
        (pltpu.VMEM((ROWS, D), f32),) * 2,
        (VMEM,) * 2,
        after=(),
        us=0.6,
    )
    came = shift(send, xh=1)

    yp, x = call(
        relay,
        place,
        [yp, x],
        [VMEM] * 2,
        (pltpu.VMEM((CHUNK, D), bf16),) * 2,
        (VMEM,) * 2,
        aliases={1: 0, 2: 1},
        us=0.1,
        after=[mine],
    )
    rows_0, pre_grad = run_hidden_grad(place, 0, [own, ym, yp, x], w, slope_0, after=[mine])
    xyp = shift(yp, xl=1)
    xym = shift(x, y=1)
    y2 = shift(yp, y=-1)
    partial, token = call(
        weight_grad_first,
        place,
        [rows_0, ht_0],
        [VMEM] * 2,
        (pltpu.VMEM((FF, D), bf16), pltpu.VMEM((8, BLOCK), f32)),
        (VMEM,) * 2,
        limit=4,
        after=(),
        us=5.6,
    )
    ht_4, slope_4 = call(
        gelu(4),
        place,
        [pre.reshape(8, CHUNK, FF)],
        [HBM],
        (pltpu.VMEM((FF, 4 * CHUNK), bf16), pltpu.VMEM((4 * CHUNK, FF), f32)),
        (VMEM,) * 2,
        [pltpu.VMEM((4, CHUNK, FF), bf16), pltpu.SemaphoreType.DMA((4,))],
        limit=6,
        us=2.8,
        after=[token],
    )
    passed = call(
        pick, place, [xym, xyp], [VMEM] * 2, pltpu.VMEM((CHUNK, D), bf16), VMEM, us=0.4, after=[slope_4]
    )
    x2 = shift(passed, y=lambda c: 1 - 2 * c)
    new_momentum, rows = call(
        outer_step,
        place,
        [mine, came, anchor.reshape(16, ROWS, D), momentum],
        [VMEM] * 4,
        (jax.ShapeDtypeStruct((ROWS, D), f32), pltpu.VMEM((ROWS, D), bf16)),
        (VMEM,) * 2,
        after=[slope_4],
        us=0.7,
    )
    near = shift(rows, xh=1)
    rows_4, pre_grad = run_hidden_grad(place, 4, [xyp, xym, y2], w, slope_4, pre_grad, after=[rows])

    pair = call(
        stack, place, [rows, near], [VMEM] * 2, pltpu.VMEM((2, ROWS, D), bf16), VMEM, us=0.4, after=[rows_4]
    )
    pairs = [pair, shift(pair, z=3), shift(pair, z=2), shift(pair, z=1)]
    (pre_grad,) = run_hidden_grad(place, 7, [x2], w, slope_4, pre_grad, after=[pair])
    mine = call(stack, place, pairs, [VMEM] * 4, pltpu.VMEM((4, 2, ROWS, D), bf16), VMEM, us=0.8, after=[pre_grad])
    other = shift(mine, c=1)
    weight_grad = call(
        weight_grad_last,
        place,
        [rows_4, x2, ht_4, partial],
        [VMEM] * 4,
        pltpu.HBM((FF, D), bf16),
        HBM,
        [pltpu.VMEM((4 * CHUNK, D), bf16), pltpu.VMEM((2, TALL, D), bf16), pltpu.SemaphoreType.DMA((2,))],
        limit=13,
        us=8.0,
        after=[mine],
    )
    new_anchor = call(
        place_rows,
        place,
        [mine, other],
        [VMEM] * 2,
        pltpu.HBM(view, bf16),
        HBM,
        [pltpu.SemaphoreType.DMA((16,))],
        us=1.5,
        after=[weight_grad],
    )
    return (
        new_anchor.reshape(1, 256, D),
        new_momentum[None],
        pre_grad.reshape(1, 8 * CHUNK, FF),
        weight_grad[None],
    )


def solution(mesh):
    return jax.shard_map(
        shards,
        mesh=mesh,
        in_specs=(
            P("shard", None, None),
            P("rep", "shard", None, None),
            P("shard", "rep", None),
            P("rep", "shard", None),
            P("rep", None, "shard"),
            P("rep", "shard", None),
        ),
        out_specs=(
            P("shard", None, None),
            P("shard", "rep", None),
            P("rep", None, "shard"),
            P("rep", "shard", None),
        ),
        check_vma=False,
    )
```

time: 311 us -> 86 us (0.28)
  waiting for transfers between devices: 223 us -> 8.95 us
  Pallas kernels: 0 us -> 46.4 us
  matrix products: 32.3 us -> 0 us
  starting transfers between devices: 0.12 us -> 28.8 us
  blocking collectives: 23.4 us -> 0 us
  between operations: 13.8 us -> 1.06 us
  other arithmetic: 11.8 us -> 0.01 us
  local copies, waits for them, and re-layouts: 6 us -> 0.73 us
    all_gather x2 -> x0, waiting for transfers between devices: 145 us -> none  [the longest x1 125 us: shards(): grad_rows = lax.all_gather(out_grad, 'shard', axis=1, tiled=True)[0]]
    reduce_scatter x1 -> x0, waiting for transfers between devices: 77.6 us -> none  [shards(): lax.psum_scatter(decode(drift_code, drift_scale), 'rep', scatter_dimensio...]
    pallas_call x0 -> x15, Pallas kernels: none -> 46.4 us  [call(): pl.pallas_call(body, out_shape=out_shape, in_specs=[SMEM, *in_specs, *aft...]
    dot_general x2 -> x0, matrix products: 32.3 us -> none  [the longest x1 16.7 us: shards(): lax.dot_general(grad_rows, weight, (((1,), (1,)), ((), ())), preferred_el...]
    ppermute x0 -> x17, starting transfers between devices: none -> 28.8 us  [shift(): return lax.ppermute(array, AXES, pairs)]
    all_gather x1 -> x0, blocking collectives: 23.4 us -> none  [shards(): lax.all_gather(step_scale, 'rep', axis=1, tiled=True)]
    ppermute x0 -> x17, waiting for transfers between devices: none -> 8.95 us  [shift(): return lax.ppermute(array, AXES, pairs)]
    convert_element_type x5 -> x0, other arithmetic: 5.79 us -> none  [the longest x1 4.65 us: shards(): (anchor.astype(jnp.float32) - outer_rate * decode(whole_code, whole_scale...]
  transfers between devices with their start and end apart: 3 -> 17, of which waited for: 3 -> 4; matrix products, arithmetic and copies ran while one was open for 2% -> 1% of each run, Pallas kernels for 0% -> 51%
where the time goes in v2:
time: 86 us; the launch traced here: 85.9 us
  Pallas kernels  46.4 us (54%)
  starting transfers between devices  28.8 us (33%)
  waiting for transfers between devices  8.95 us (10%)
  between operations  1.06 us (1%)
    pallas_call x15, Pallas kernels, call(): pl.pallas_call(body, out_shape=out_shape, in_specs=[SMEM, *in_specs, *aft...  46.4 us
    ppermute x17, starting transfers between devices, shift(): return lax.ppermute(array, AXES, pairs)  28.8 us
    ppermute x17, waiting for transfers between devices, shift(): return lax.ppermute(array, AXES, pairs)  8.95 us
  transfers between devices with their start and end apart: 17, of which 4 were waited for; matrix products, arithmetic and copies ran while one was open for 1% of the time, Pallas kernels for 51%

profile of v2, /device:TPU:1, one launch (start us, length us, event | category | flops | bytes accessed | tf_op | source)
XLA Modules:
  0.0 85.9 jit_solution(9834465108239140782)
XLA Ops:
  0.6 1.5 %collective-permute-start = (bf16[2,4,32,3072]{3,2,1,0:T(8,128)(2,1)}, bf16[2,4,32,3072]{3,2,1,0:T(8,128)(2,1)}, u32[]{:S(2)}, u32[]{:S(2)}) collective-permute-start(bf16[2,4,32,3072]{3,2,1,0:T(8,128)(2,1)} %bitcast.30), channel_id=1, source_target_pairs={{0,8},{1,9},{2,10},{3,11},{4,12},{5,13},{6,14},{7,15},{8,0},{9,1},... | collective-permute-start | bytes 4718600 | tf_op jit(solution)/shard_map/ppermute | solution.py:43
  2.1 1.3 %collective-permute-start.7 = (bf16[128,3072]{1,0:T(8,128)(2,1)}, bf16[128,3072]{1,0:T(8,128)(2,1)S(1)}, u32[]{:S(2)}, u32[]{:S(2)}) collective-permute-start(bf16[128,3072]{1,0:T(8,128)(2,1)} %bitcast.21), channel_id=1, source_target_pairs={{0,1},{1,0},{2,3},{3,2},{4,5},{5,4},{6,7},{7,6},{8,9},{9,8},{10,11... | collective-permute-start | bytes 2359304 | tf_op jit(solution)/shard_map/ppermute | solution.py:43
  3.4 2.7 %collective-permute-start.6 = (bf16[128,3072]{1,0:T(8,128)(2,1)}, bf16[128,3072]{1,0:T(8,128)(2,1)S(1)}, u32[]{:S(2)}, u32[]{:S(2)}) collective-permute-start(bf16[128,3072]{1,0:T(8,128)(2,1)} %bitcast.22), channel_id=1, source_target_pairs={{0,6},{1,7},{2,0},{3,1},{4,2},{5,3},{6,4},{7,5},{8,14},{9,15},{10,... | collective-permute-start | bytes 2359304 | tf_op jit(solution)/shard_map/ppermute | solution.py:43
  6.2 0.7 dynamic-slice_bitcast_fusion.place
  6.9 4.1 %gelu_0.1 = (bf16[1536,512]{1,0:T(8,128)(2,1)S(1)}, f32[512,1536]{1,0:T(8,128)S(1)}) custom-call(s32[12]{0:T(128)S(1)} %dynamic-slice_bitcast_fusion.place, bf16[8,128,1536]{2,1,0:T(8,128)(2,1)} %bitcast.28), custom_call_target="tpu_custom_call" | custom-call | flops 2800000000 | tf_op jit(solution)/shard_map/gelu_0/pallas_call | solution.py:69
  11.0 0.0 collective-permute-done.refs_2_
  11.0 0.0 slice-start.2
  11.0 3.5 %drift_sums.1 = (f32[2,16,3072]{2,1,0:T(8,128)S(1)}, bf16[2,16,3072]{2,1,0:T(8,128)(2,1)S(1)}, bf16[2,16,3072]{2,1,0:T(8,128)(2,1)S(1)}, bf16[2,16,3072]{2,1,0:T(8,128)(2,1)S(1)}) custom-call(s32[12]{0:T(128)S(1)} %dynamic-slice_bitcast_fusion.place, bf16[2,4,32,3072]{3,2,1,0:T(8,128)(2,1)} %bitcast.18, bf16[2,4,32,3072]{3,2,1,0:T(8,128)(2,1)} %bitcast.31, ...), custom_call_target="tpu_custom_call" | custom-call | flops 3000000000 | tf_op jit(solution)/shard_map/drift_sums/pallas_call | solution.py:69
  14.5 0.0 copy-start.2
  14.5 1.7 %collective-permute-start.1 = (bf16[2,16,3072]{2,1,0:T(8,128)(2,1)S(1)}, bf16[2,16,3072]{2,1,0:T(8,128)(2,1)S(1)}, u32[]{:S(2)}, u32[]{:S(2)}) collective-permute-start(bf16[2,16,3072]{2,1,0:T(8,128)(2,1)S(1)} %get-tuple-element.26), channel_id=1, source_target_pairs={{0,16},{1,17},{2,18},{3,19},{4,20},{5,21},{6,22},{7,23},{8,24},{9,... | collective-permute-start | bytes 589832 | tf_op jit(solution)/shard_map/ppermute | solution.py:43
  16.3 3.3 %collective-permute-start.2 = (bf16[2,16,3072]{2,1,0:T(8,128)(2,1)S(1)}, bf16[2,16,3072]{2,1,0:T(8,128)(2,1)S(1)}, u32[]{:S(2)}, u32[]{:S(2)}) collective-permute-start(bf16[2,16,3072]{2,1,0:T(8,128)(2,1)S(1)} %get-tuple-element.27), channel_id=1, source_target_pairs={{0,32},{1,33},{2,34},{3,35},{4,36},{5,37},{6,38},{7,39},{8,40},{9,... | collective-permute-start | bytes 589832 | tf_op jit(solution)/shard_map/ppermute | solution.py:43
  19.6 3.5 %collective-permute-done.1.refs_1_ = bf16[2,16,3072]{2,1,0:T(8,128)(2,1)S(1)} collective-permute-done((bf16[2,16,3072]{2,1,0:T(8,128)(2,1)S(1)}, bf16[2,16,3072]{2,1,0:T(8,128)(2,1)S(1)}, u32[]{:S(2)}, u32[]{:S(2)}) %collective-permute-start.1) | collective-permute-done | bytes 196640 | tf_op jit(solution)/shard_map/ppermute | solution.py:43
  23.0 1.1 %collective-permute-start.3 = (bf16[2,16,3072]{2,1,0:T(8,128)(2,1)S(1)}, bf16[2,16,3072]{2,1,0:T(8,128)(2,1)S(1)}, u32[]{:S(2)}, u32[]{:S(2)}) collective-permute-start(bf16[2,16,3072]{2,1,0:T(8,128)(2,1)S(1)} %get-tuple-element.28), channel_id=1, source_target_pairs={{0,48},{1,49},{2,50},{3,51},{4,52},{5,53},{6,54},{7,55},{8,56},{9,... | collective-permute-start | bytes 589832 | tf_op jit(solution)/shard_map/ppermute | solution.py:43
  24.2 3.9 %collective-permute-done.2.refs_2_ = bf16[2,16,3072]{2,1,0:T(8,128)(2,1)S(1)} collective-permute-done((bf16[2,16,3072]{2,1,0:T(8,128)(2,1)S(1)}, bf16[2,16,3072]{2,1,0:T(8,128)(2,1)S(1)}, u32[]{:S(2)}, u32[]{:S(2)}) %collective-permute-start.2) | collective-permute-done | bytes 196640 | tf_op jit(solution)/shard_map/ppermute | solution.py:43
  28.1 0.6 z_sums.1
  28.8 0.0 collective-permute-done.6.refs_0_
  28.8 0.5 relay.1
  29.3 2.4 %collective-permute-start.11 = (bf16[128,3072]{1,0:T(8,128)(2,1)S(1)}, bf16[128,3072]{1,0:T(8,128)(2,1)S(1)}, u32[]{:S(2)}, u32[]{:S(2)}) collective-permute-start(bf16[128,3072]{1,0:T(8,128)(2,1)S(1)} %get-tuple-element.31.refs_2_), channel_id=1, source_target_pairs={{0,6},{1,7},{2,0},{3,1},{4,2},{5,3},{6,4},{7,5},{8,14},{9,15},{10,... | collective-permute-start | bytes 2359304 | tf_op jit(solution)/shard_map/ppermute | solution.py:43
  31.7 0.3 collective-permute-start.9
  32.0 2.7 %collective-permute-start.4 = (f32[16,3072]{1,0:T(8,128)S(1)}, f32[16,3072]{1,0:T(8,128)S(1)}, u32[]{:S(2)}, u32[]{:S(2)}) collective-permute-start(f32[16,3072]{1,0:T(8,128)S(1)} %get-tuple-element.30), channel_id=1, source_target_pairs={{0,64},{1,65},{2,66},{3,67},{4,68},{5,69},{6,70},{7,71},{8,72},{9,... | collective-permute-start | bytes 589832 | tf_op jit(solution)/shard_map/ppermute | solution.py:43
  34.7 0.0 collective-permute-start.10
  34.8 6.5 %hidden_grad_0.1 = (bf16[512,3072]{1,0:T(8,128)(2,1)S(1)}, bf16[8,128,1536]{2,1,0:T(8,128)(2,1)}) custom-call(s32[12]{0:T(128)S(1)} %dynamic-slice_bitcast_fusion.place, bf16[128,3072]{1,0:T(8,128)(2,1)S(1)} %bitcast.24, bf16[128,3072]{1,0:T(8,128)(2,1)S(1)} %collective-permute-done.5.refs_1_, bf16[128,3072]{1,0:T(8,128)(2,1)S(1)} %get-tuple-element.31.refs_2_, ...), custom_call_target="tpu_custom_call" | custom-call | flops 6700000256 | tf_op jit(solution)/shard_map/hidden_grad_0/pallas_call | solution.py:69
  41.3 5.7 %weight_grad_first.1 = (bf16[1536,3072]{1,0:T(8,128)(2,1)S(1)}, f32[8,128]{1,0:T(8,128)S(1)}) custom-call(s32[12]{0:T(128)S(1)} %dynamic-slice_bitcast_fusion.place, bf16[512,3072]{1,0:T(8,128)(2,1)S(1)} %get-tuple-element.33.refs_0_, bf16[1536,512]{1,0:T(8,128)(2,1)S(1)} %get-tuple-element.34.refs_1_), custom_call_target="tpu_custom_call" | custom-call | flops 5600000000 | tf_op jit(solution)/shard_map/weight_grad_first/pallas_call | solution.py:69
  47.0 3.8 %gelu_4.1 = (bf16[1536,512]{1,0:T(8,128)(2,1)S(1)}, f32[512,1536]{1,0:T(8,128)S(1)}) custom-call(s32[12]{0:T(128)S(1)} %dynamic-slice_bitcast_fusion.place, bf16[8,128,1536]{2,1,0:T(8,128)(2,1)} %bitcast.29, f32[8,128]{1,0:T(8,128)S(1)} %get-tuple-element.35.refs_1_), custom_call_target="tpu_custom_call" | custom-call | flops 2800000000 | tf_op jit(solution)/shard_map/gelu_4/pallas_call | solution.py:69
  50.9 0.0 copy-start
  50.9 0.0 copy-start.1
  50.9 0.0 collective-permute-done.10.refs_1_.refs_0_
  50.9 0.6 pick.1
  51.5 2.7 %collective-permute-start.15 = (bf16[128,3072]{1,0:T(8,128)(2,1)S(1)}, bf16[128,3072]{1,0:T(8,128)(2,1)S(1)}, u32[]{:S(2)}, u32[]{:S(2)}) collective-permute-start(bf16[128,3072]{1,0:T(8,128)(2,1)S(1)} %pick.1), channel_id=1, source_target_pairs={{0,2},{1,3},{2,4},{3,5},{4,6},{5,7},{6,0},{7,1},{8,14},{9,15},{10,... | collective-permute-start | bytes 2359304 | tf_op jit(solution)/shard_map/ppermute | solution.py:43
  54.3 1.3 %outer_step.1 = (f32[16,3072]{1,0:T(8,128)}, bf16[16,3072]{1,0:T(8,128)(2,1)S(1)}) custom-call(s32[12]{0:T(128)S(1)} %dynamic-slice_bitcast_fusion.place, f32[16,3072]{1,0:T(8,128)S(1)} %get-tuple-element.29.refs_2_.refs_6_.refs_0_, f32[16,3072]{1,0:T(8,128)S(1)} %collective-permute-done.4.refs_1_, bf16[16,16,3072]{2,1,0:T(8,128)(2,1)S(1)} %bitcast.19, ...), custom_call_target="tpu_custom_call" | custom-call | flops 700000000 | tf_op jit(solution)/shard_map/outer_step/pallas_call | solution.py:69
  55.5 0.2 collective-permute-start.8
  55.8 0.0 collective-permute-done.11.refs_2_
  55.8 5.2 %hidden_grad_4.1 = (bf16[384,3072]{1,0:T(8,128)(2,1)S(1)}, bf16[8,128,1536]{2,1,0:T(8,128)(2,1)}) custom-call(s32[12]{0:T(128)S(1)} %dynamic-slice_bitcast_fusion.place, bf16[128,3072]{1,0:T(8,128)(2,1)S(1)} %collective-permute-done.9.refs_0_.refs_1_, bf16[128,3072]{1,0:T(8,128)(2,1)S(1)} %collective-permute-done.10.refs_1_.refs_0_, ...), custom_call_target="tpu_custom_call", output_to_operand_aliasing={{1}: (6, {})} | custom-call | flops 5400000000 | tf_op jit(solution)/shard_map/hidden_grad_4/pallas_call | solution.py:69
  61.0 0.0 collective-permute-done.8.refs_1_
  61.0 0.6 stack.2.refs_4_.refs_0_
  61.6 0.4 collective-permute-start.14
  62.0 2.6 %collective-permute-start.13 = (bf16[2,16,3072]{2,1,0:T(8,128)(2,1)S(1)}, bf16[2,16,3072]{2,1,0:T(8,128)(2,1)S(1)}, u32[]{:S(2)}, u32[]{:S(2)}) collective-permute-start(bf16[2,16,3072]{2,1,0:T(8,128)(2,1)S(1)} %stack.2.refs_4_.refs_0_), channel_id=1, source_target_pairs={{0,32},{1,33},{2,34},{3,35},{4,36},{5,37},{6,38},{7,39},{8,40},{9,... | collective-permute-start | bytes 589832 | tf_op jit(solution)/shard_map/ppermute | solution.py:43
  64.6 0.3 collective-permute-start.12
  64.9 0.0 collective-permute-done.15.refs_0_.refs_1_
  64.9 3.9 %hidden_grad_7.1.refs_4_ = bf16[8,128,1536]{2,1,0:T(8,128)(2,1)} custom-call(s32[12]{0:T(128)S(1)} %dynamic-slice_bitcast_fusion.place, bf16[128,3072]{1,0:T(8,128)(2,1)S(1)} %collective-permute-done.15.refs_0_.refs_1_, bf16[1536,3072]{1,0:T(8,128)(2,1)S(1)} %bitcast.17, ...), custom_call_target="tpu_custom_call", output_to_operand_aliasing={{}: (4, {})} | custom-call | flops 2800000000 | tf_op jit(solution)/shard_map/hidden_grad_7/pallas_call | solution.py:69
  68.9 0.0 collective-permute-done.14.refs_3_
  68.9 0.9 %collective-permute-done.13.refs_2_ = bf16[2,16,3072]{2,1,0:T(8,128)(2,1)S(1)} collective-permute-done((bf16[2,16,3072]{2,1,0:T(8,128)(2,1)S(1)}, bf16[2,16,3072]{2,1,0:T(8,128)(2,1)S(1)}, u32[]{:S(2)}, u32[]{:S(2)}) %collective-permute-start.13) | collective-permute-done | bytes 196640 | tf_op jit(solution)/shard_map/ppermute | solution.py:43
  69.8 0.6 collective-permute-done.12.refs_1_
  70.4 0.6 stack.3.refs_4_.refs_0_
  71.0 5.3 %collective-permute-start.16 = (bf16[4,2,16,3072]{3,2,1,0:T(8,128)(2,1)S(1)}, bf16[4,2,16,3072]{3,2,1,0:T(8,128)(2,1)S(1)}, u32[]{:S(2)}, u32[]{:S(2)}) collective-permute-start(bf16[4,2,16,3072]{3,2,1,0:T(8,128)(2,1)S(1)} %stack.3.refs_4_.refs_0_), channel_id=1, source_target_pairs={{0,8},{1,9},{2,10},{3,11},{4,12},{5,13},{6,14},{7,15},{8,0},{9,1},... | collective-permute-start | bytes 2359304 | tf_op jit(solution)/shard_map/ppermute | solution.py:43
  76.3 7.5 %weight_grad_last.1.refs_2_ = bf16[1536,3072]{1,0:T(8,128)(2,1)} custom-call(s32[12]{0:T(128)S(1)} %dynamic-slice_bitcast_fusion.place, bf16[384,3072]{1,0:T(8,128)(2,1)S(1)} %get-tuple-element.39.refs_2_.refs_0_, bf16[128,3072]{1,0:T(8,128)(2,1)S(1)} %collective-permute-done.15.refs_0_.refs_1_, bf16[1536,512]{1,0:T(8,128)(2,1)S(1)} %get-tuple-element.41.refs_2_, ...), custom_call_target="tpu_custom_call" | custom-call | flops 8000000000 | tf_op jit(solution)/shard_map/weight_grad_last/pallas_call | solution.py:69
  83.9 0.0 collective-permute-done.16.refs_1_
  83.9 1.8 %place_rows.1 = bf16[2,4,32,3072]{3,2,1,0:T(8,128)(2,1)} custom-call(s32[12]{0:T(128)S(1)} %dynamic-slice_bitcast_fusion.place, bf16[4,2,16,3072]{3,2,1,0:T(8,128)(2,1)S(1)} %stack.3.refs_4_.refs_0_, bf16[4,2,16,3072]{3,2,1,0:T(8,128)(2,1)S(1)} %collective-permute-done.16.refs_1_, bf16[1536,3072]{1,0:T(8,128)(2,1)} %weight_grad_last.1.refs_2_), custom_call_target="tpu_custom_call" | custom-call | flops 1500000000 | tf_op jit(solution)/shard_map/place_rows/pallas_call | solution.py:69
  (15 shorter events, 0.0 us)
Async XLA Ops:
  0.6 10.4 %collective-permute-start = (bf16[2,4,32,3072]{3,2,1,0:T(8,128)(2,1)}, bf16[2,4,32,3072]{3,2,1,0:T(8,128)(2,1)}, u32[]{:S(2)}, u32[]{:S(2)}) collective-permute-start(bf16[2,4,32,3072]{3,2,1,0:T(8,128)(2,1)} %bitcast.30), channel_id=1, source_target_pairs={{0,8},{1,9},{2,10},{3,11},{4,12},{5,13},{6,14},{7,15},{8,0},{9,1},... | collective-permute-start | bytes 4718600 | tf_op jit(solution)/shard_map/ppermute | solution.py:43
  2.1 26.6 %collective-permute-start.7 = (bf16[128,3072]{1,0:T(8,128)(2,1)}, bf16[128,3072]{1,0:T(8,128)(2,1)S(1)}, u32[]{:S(2)}, u32[]{:S(2)}) collective-permute-start(bf16[128,3072]{1,0:T(8,128)(2,1)} %bitcast.21), channel_id=1, source_target_pairs={{0,1},{1,0},{2,3},{3,2},{4,5},{5,4},{6,7},{7,6},{8,9},{9,8},{10,11... | collective-permute-start | bytes 2359304 | tf_op jit(solution)/shard_map/ppermute | solution.py:43
  3.4 25.3 %collective-permute-start.6 = (bf16[128,3072]{1,0:T(8,128)(2,1)}, bf16[128,3072]{1,0:T(8,128)(2,1)S(1)}, u32[]{:S(2)}, u32[]{:S(2)}) collective-permute-start(bf16[128,3072]{1,0:T(8,128)(2,1)} %bitcast.22), channel_id=1, source_target_pairs={{0,6},{1,7},{2,0},{3,1},{4,2},{5,3},{6,4},{7,5},{8,14},{9,15},{10,... | collective-permute-start | bytes 2359304 | tf_op jit(solution)/shard_map/ppermute | solution.py:43
  6.2 28.6 %collective-permute-start.5 = (bf16[128,3072]{1,0:T(8,128)(2,1)}, bf16[128,3072]{1,0:T(8,128)(2,1)S(1)}, u32[]{:S(2)}, u32[]{:S(2)}) collective-permute-start(bf16[128,3072]{1,0:T(8,128)(2,1)} %bitcast.23), channel_id=1, source_target_pairs={{0,2},{1,3},{2,4},{3,5},{4,6},{5,7},{6,0},{7,1},{8,10},{9,11},{10,... | collective-permute-start | bytes 2359304 | tf_op jit(solution)/shard_map/ppermute | solution.py:43
  6.9 27.9 %slice-start = ((s8[9437184]{0:T(1024)(128)(4,1)}), s8[4194304]{0:T(1024)(128)(4,1)S(1)}, s32[]{:S(2)}) async-start(s8[9437184]{0:T(1024)(128)(4,1)} %bitcast.13), calls=%async_computation | async-start | bytes 8388608
  6.9 27.9 %slice-start.1 = ((s8[9437184]{0:T(1024)(128)(4,1)}), s8[4194304]{0:T(1024)(128)(4,1)S(1)}, s32[]{:S(2)}) async-start(s8[9437184]{0:T(1024)(128)(4,1)} %bitcast.13), calls=%async_computation.1 | async-start | bytes 8388608
  11.0 23.8 %slice-start.2 = ((s8[9437184]{0:T(1024)(128)(4,1)}), s8[1048576]{0:T(1024)(128)(4,1)S(1)}, s32[]{:S(2)}) async-start(s8[9437184]{0:T(1024)(128)(4,1)} %bitcast.13), calls=%async_computation.2 | async-start | bytes 2097152
  14.5 20.2 %copy-start.2 = (bf16[1,128,3072]{2,1,0:T(8,128)(2,1)S(1)}, bf16[1,128,3072]{2,1,0:T(8,128)(2,1)}, u32[]{:S(2)}) copy-start(bf16[1,128,3072]{2,1,0:T(8,128)(2,1)} %param.10) | copy-start | bytes 2359300
  14.5 8.5 %collective-permute-start.1 = (bf16[2,16,3072]{2,1,0:T(8,128)(2,1)S(1)}, bf16[2,16,3072]{2,1,0:T(8,128)(2,1)S(1)}, u32[]{:S(2)}, u32[]{:S(2)}) collective-permute-start(bf16[2,16,3072]{2,1,0:T(8,128)(2,1)S(1)} %get-tuple-element.26), channel_id=1, source_target_pairs={{0,16},{1,17},{2,18},{3,19},{4,20},{5,21},{6,22},{7,23},{8,24},{9,... | collective-permute-start | bytes 589832 | tf_op jit(solution)/shard_map/ppermute | solution.py:43
  16.3 11.9 %collective-permute-start.2 = (bf16[2,16,3072]{2,1,0:T(8,128)(2,1)S(1)}, bf16[2,16,3072]{2,1,0:T(8,128)(2,1)S(1)}, u32[]{:S(2)}, u32[]{:S(2)}) collective-permute-start(bf16[2,16,3072]{2,1,0:T(8,128)(2,1)S(1)} %get-tuple-element.27), channel_id=1, source_target_pairs={{0,32},{1,33},{2,34},{3,35},{4,36},{5,37},{6,38},{7,39},{8,40},{9,... | collective-permute-start | bytes 589832 | tf_op jit(solution)/shard_map/ppermute | solution.py:43
  23.0 5.1 %collective-permute-start.3 = (bf16[2,16,3072]{2,1,0:T(8,128)(2,1)S(1)}, bf16[2,16,3072]{2,1,0:T(8,128)(2,1)S(1)}, u32[]{:S(2)}, u32[]{:S(2)}) collective-permute-start(bf16[2,16,3072]{2,1,0:T(8,128)(2,1)S(1)} %get-tuple-element.28), channel_id=1, source_target_pairs={{0,48},{1,49},{2,50},{3,51},{4,52},{5,53},{6,54},{7,55},{8,56},{9,... | collective-permute-start | bytes 589832 | tf_op jit(solution)/shard_map/ppermute | solution.py:43
  29.3 26.5 %collective-permute-start.11 = (bf16[128,3072]{1,0:T(8,128)(2,1)S(1)}, bf16[128,3072]{1,0:T(8,128)(2,1)S(1)}, u32[]{:S(2)}, u32[]{:S(2)}) collective-permute-start(bf16[128,3072]{1,0:T(8,128)(2,1)S(1)} %get-tuple-element.31.refs_2_), channel_id=1, source_target_pairs={{0,6},{1,7},{2,0},{3,1},{4,2},{5,3},{6,4},{7,5},{8,14},{9,15},{10,... | collective-permute-start | bytes 2359304 | tf_op jit(solution)/shard_map/ppermute | solution.py:43
  31.7 19.2 %collective-permute-start.9 = (bf16[128,3072]{1,0:T(8,128)(2,1)S(1)}, bf16[128,3072]{1,0:T(8,128)(2,1)S(1)}, u32[]{:S(2)}, u32[]{:S(2)}) collective-permute-start(bf16[128,3072]{1,0:T(8,128)(2,1)S(1)} %get-tuple-element.31.refs_2_), channel_id=1, source_target_pairs={{0,1},{1,0},{2,3},{3,2},{4,5},{5,4},{6,7},{7,6},{8,9},{9,8},{10,11... | collective-permute-start | bytes 2359304 | tf_op jit(solution)/shard_map/ppermute | solution.py:43
  32.0 22.3 %collective-permute-start.4 = (f32[16,3072]{1,0:T(8,128)S(1)}, f32[16,3072]{1,0:T(8,128)S(1)}, u32[]{:S(2)}, u32[]{:S(2)}) collective-permute-start(f32[16,3072]{1,0:T(8,128)S(1)} %get-tuple-element.30), channel_id=1, source_target_pairs={{0,64},{1,65},{2,66},{3,67},{4,68},{5,69},{6,70},{7,71},{8,72},{9,... | collective-permute-start | bytes 589832 | tf_op jit(solution)/shard_map/ppermute | solution.py:43
  34.7 16.2 %collective-permute-start.10 = (bf16[128,3072]{1,0:T(8,128)(2,1)S(1)}, bf16[128,3072]{1,0:T(8,128)(2,1)S(1)}, u32[]{:S(2)}, u32[]{:S(2)}) collective-permute-start(bf16[128,3072]{1,0:T(8,128)(2,1)S(1)} %get-tuple-element.32.refs_3_), channel_id=1, source_target_pairs={{0,2},{1,3},{2,4},{3,5},{4,6},{5,7},{6,0},{7,1},{8,10},{9,11},{10,... | collective-permute-start | bytes 2359304 | tf_op jit(solution)/shard_map/ppermute | solution.py:43
  50.9 3.4 %copy-start = (bf16[1,256,3072]{2,1,0:T(8,128)(2,1)S(1)}, bf16[1,256,3072]{2,1,0:T(8,128)(2,1)}, u32[]{:S(2)}) copy-start(bf16[1,256,3072]{2,1,0:T(8,128)(2,1)} %param.7) | copy-start | bytes 4718596
  50.9 3.4 %copy-start.1 = (f32[1,16,3072]{2,1,0:T(8,128)S(1)}, f32[1,16,3072]{2,1,0:T(8,128)}, u32[]{:S(2)}) copy-start(f32[1,16,3072]{2,1,0:T(8,128)} %param.9) | copy-start | bytes 589828
  51.5 13.4 %collective-permute-start.15 = (bf16[128,3072]{1,0:T(8,128)(2,1)S(1)}, bf16[128,3072]{1,0:T(8,128)(2,1)S(1)}, u32[]{:S(2)}, u32[]{:S(2)}) collective-permute-start(bf16[128,3072]{1,0:T(8,128)(2,1)S(1)} %pick.1), channel_id=1, source_target_pairs={{0,2},{1,3},{2,4},{3,5},{4,6},{5,7},{6,0},{7,1},{8,14},{9,15},{10,... | collective-permute-start | bytes 2359304 | tf_op jit(solution)/shard_map/ppermute | solution.py:43
  55.5 5.5 %collective-permute-start.8 = (bf16[16,3072]{1,0:T(8,128)(2,1)S(1)}, bf16[16,3072]{1,0:T(8,128)(2,1)S(1)}, u32[]{:S(2)}, u32[]{:S(2)}) collective-permute-start(bf16[16,3072]{1,0:T(8,128)(2,1)S(1)} %get-tuple-element.37.refs_6_.refs_0_), channel_id=1, source_target_pairs={{0,64},{1,65},{2,66},{3,67},{4,68},{5,69},{6,70},{7,71},{8,72},{9,... | collective-permute-start | bytes 294920 | tf_op jit(solution)/shard_map/ppermute | solution.py:43
  61.6 7.3 %collective-permute-start.14 = (bf16[2,16,3072]{2,1,0:T(8,128)(2,1)S(1)}, bf16[2,16,3072]{2,1,0:T(8,128)(2,1)S(1)}, u32[]{:S(2)}, u32[]{:S(2)}) collective-permute-start(bf16[2,16,3072]{2,1,0:T(8,128)(2,1)S(1)} %stack.2.refs_4_.refs_0_), channel_id=1, source_target_pairs={{0,16},{1,17},{2,18},{3,19},{4,20},{5,21},{6,22},{7,23},{8,24},{9,... | collective-permute-start | bytes 589832 | tf_op jit(solution)/shard_map/ppermute | solution.py:43
  62.0 7.8 %collective-permute-start.13 = (bf16[2,16,3072]{2,1,0:T(8,128)(2,1)S(1)}, bf16[2,16,3072]{2,1,0:T(8,128)(2,1)S(1)}, u32[]{:S(2)}, u32[]{:S(2)}) collective-permute-start(bf16[2,16,3072]{2,1,0:T(8,128)(2,1)S(1)} %stack.2.refs_4_.refs_0_), channel_id=1, source_target_pairs={{0,32},{1,33},{2,34},{3,35},{4,36},{5,37},{6,38},{7,39},{8,40},{9,... | collective-permute-start | bytes 589832 | tf_op jit(solution)/shard_map/ppermute | solution.py:43
  64.6 5.8 %collective-permute-start.12 = (bf16[2,16,3072]{2,1,0:T(8,128)(2,1)S(1)}, bf16[2,16,3072]{2,1,0:T(8,128)(2,1)S(1)}, u32[]{:S(2)}, u32[]{:S(2)}) collective-permute-start(bf16[2,16,3072]{2,1,0:T(8,128)(2,1)S(1)} %stack.2.refs_4_.refs_0_), channel_id=1, source_target_pairs={{0,48},{1,49},{2,50},{3,51},{4,52},{5,53},{6,54},{7,55},{8,56},{9,... | collective-permute-start | bytes 589832 | tf_op jit(solution)/shard_map/ppermute | solution.py:43
  71.0 12.9 %collective-permute-start.16 = (bf16[4,2,16,3072]{3,2,1,0:T(8,128)(2,1)S(1)}, bf16[4,2,16,3072]{3,2,1,0:T(8,128)(2,1)S(1)}, u32[]{:S(2)}, u32[]{:S(2)}) collective-permute-start(bf16[4,2,16,3072]{3,2,1,0:T(8,128)(2,1)S(1)} %stack.3.refs_4_.refs_0_), channel_id=1, source_target_pairs={{0,8},{1,9},{2,10},{3,11},{4,12},{5,13},{6,14},{7,15},{8,0},{9,1},... | collective-permute-start | bytes 2359304 | tf_op jit(solution)/shard_map/ppermute | solution.py:43

commit v3 on v2

--- a/solution.py
+++ b/solution.py
@@ -169,10 +169,12 @@
 def gelu(first):
     def kernel(place, pre, hidden_t, slope, held, sems):
         copies = [pltpu.make_async_copy(pre.at[place[first + i]], held.at[i], sems.at[i]) for i in range(4)]
-        for copy in copies:
-            copy.start()
+        copies[0].start()
+        copies[1].start()
         for i, copy in enumerate(copies):
             copy.wait()
+            if i < 2:
+                copies[i + 2].start()
             here = slice(i * CHUNK, (i + 1) * CHUNK)
             for j in range(FF // WIDTH):
                 cols = slice(j * WIDTH, (j + 1) * WIDTH)
@@ -345,7 +347,7 @@
         (VMEM,) * 2,
         aliases={1: 0, 2: 1},
         us=0.1,
-        after=[mine],
+        after=[kept],
     )
     rows_0, pre_grad = run_hidden_grad(place, 0, [own, ym, yp, x], w, slope_0, after=[mine])
     xyp = shift(yp, xl=1)
@@ -377,7 +379,7 @@
     passed = call(
         pick, place, [xym, xyp], [VMEM] * 2, pltpu.VMEM((CHUNK, D), bf16), VMEM, us=0.4, after=[slope_4]
     )
-    x2 = shift(passed, y=lambda c: 1 - 2 * c)
+    x2 = shift(passed, y=lambda core: 1 - 2 * core)
     new_momentum, rows = call(
         outer_step,
         place,

time: 86 us -> 84.2 us (0.979)
  waiting for transfers between devices: 8.95 us -> 4.21 us
  starting transfers between devices: 28.8 us -> 31.1 us
    ppermute x17, waiting for transfers between devices: 8.95 us -> 4.21 us  [shift(): return lax.ppermute(array, AXES, pairs)]
    ppermute x17, starting transfers between devices: 28.8 us -> 31.1 us  [shift(): return lax.ppermute(array, AXES, pairs)]
  transfers between devices with their start and end apart: 17 -> 17, of which waited for: 4 -> 2; matrix products, arithmetic and copies ran while one was open for 1% -> 1% of each run, Pallas kernels for 51% -> 53%
where the time goes in v3:
time: 84.2 us; the launch traced here: 84 us
  Pallas kernels  46.9 us (56%)
  starting transfers between devices  31.1 us (37%)
  waiting for transfers between devices  4.21 us (5%)
  between operations  1.04 us (1%)
    pallas_call x15, Pallas kernels, call(): pl.pallas_call(body, out_shape=out_shape, in_specs=[SMEM, *in_specs, *aft...  46.9 us
    ppermute x17, starting transfers between devices, shift(): return lax.ppermute(array, AXES, pairs)  31.1 us
    ppermute x17, waiting for transfers between devices, shift(): return lax.ppermute(array, AXES, pairs)  4.21 us
  transfers between devices with their start and end apart: 17, of which 2 were waited for; matrix products, arithmetic and copies ran while one was open for 1% of the time, Pallas kernels for 53%

profile of v3, /device:TPU:1, one launch (start us, length us, event | category | flops | bytes accessed | tf_op | source)
XLA Modules:
  0.0 84.0 jit_solution(5692673558307349702)
XLA Ops:
  0.6 1.5 %collective-permute-start = (bf16[2,4,32,3072]{3,2,1,0:T(8,128)(2,1)}, bf16[2,4,32,3072]{3,2,1,0:T(8,128)(2,1)}, u32[]{:S(2)}, u32[]{:S(2)}) collective-permute-start(bf16[2,4,32,3072]{3,2,1,0:T(8,128)(2,1)} %bitcast.30), channel_id=1, source_target_pairs={{0,8},{1,9},{2,10},{3,11},{4,12},{5,13},{6,14},{7,15},{8,0},{9,1},... | collective-permute-start | bytes 4718600 | tf_op jit(solution)/shard_map/ppermute | solution.py:43
  2.1 1.3 %collective-permute-start.7 = (bf16[128,3072]{1,0:T(8,128)(2,1)}, bf16[128,3072]{1,0:T(8,128)(2,1)S(1)}, u32[]{:S(2)}, u32[]{:S(2)}) collective-permute-start(bf16[128,3072]{1,0:T(8,128)(2,1)} %bitcast.21), channel_id=1, source_target_pairs={{0,1},{1,0},{2,3},{3,2},{4,5},{5,4},{6,7},{7,6},{8,9},{9,8},{10,11... | collective-permute-start | bytes 2359304 | tf_op jit(solution)/shard_map/ppermute | solution.py:43
  3.4 2.7 %collective-permute-start.6 = (bf16[128,3072]{1,0:T(8,128)(2,1)}, bf16[128,3072]{1,0:T(8,128)(2,1)S(1)}, u32[]{:S(2)}, u32[]{:S(2)}) collective-permute-start(bf16[128,3072]{1,0:T(8,128)(2,1)} %bitcast.22), channel_id=1, source_target_pairs={{0,6},{1,7},{2,0},{3,1},{4,2},{5,3},{6,4},{7,5},{8,14},{9,15},{10,... | collective-permute-start | bytes 2359304 | tf_op jit(solution)/shard_map/ppermute | solution.py:43
  6.2 0.7 dynamic-slice_bitcast_fusion.place
  6.9 4.7 %gelu_0.1 = (bf16[1536,512]{1,0:T(8,128)(2,1)S(1)}, f32[512,1536]{1,0:T(8,128)S(1)}) custom-call(s32[12]{0:T(128)S(1)} %dynamic-slice_bitcast_fusion.place, bf16[8,128,1536]{2,1,0:T(8,128)(2,1)} %bitcast.28), custom_call_target="tpu_custom_call" | custom-call | flops 2800000000 | tf_op jit(solution)/shard_map/gelu_0/pallas_call | solution.py:69
  11.6 0.0 slice-start.2
  11.7 3.5 %drift_sums.1 = (f32[2,16,3072]{2,1,0:T(8,128)S(1)}, bf16[2,16,3072]{2,1,0:T(8,128)(2,1)S(1)}, bf16[2,16,3072]{2,1,0:T(8,128)(2,1)S(1)}, bf16[2,16,3072]{2,1,0:T(8,128)(2,1)S(1)}) custom-call(s32[12]{0:T(128)S(1)} %dynamic-slice_bitcast_fusion.place, bf16[2,4,32,3072]{3,2,1,0:T(8,128)(2,1)} %bitcast.18, bf16[2,4,32,3072]{3,2,1,0:T(8,128)(2,1)} %bitcast.31, ...), custom_call_target="tpu_custom_call" | custom-call | flops 3000000000 | tf_op jit(solution)/shard_map/drift_sums/pallas_call | solution.py:69
  15.2 0.0 copy-start.2
  15.2 1.7 %collective-permute-start.1 = (bf16[2,16,3072]{2,1,0:T(8,128)(2,1)S(1)}, bf16[2,16,3072]{2,1,0:T(8,128)(2,1)S(1)}, u32[]{:S(2)}, u32[]{:S(2)}) collective-permute-start(bf16[2,16,3072]{2,1,0:T(8,128)(2,1)S(1)} %get-tuple-element.26), channel_id=1, source_target_pairs={{0,16},{1,17},{2,18},{3,19},{4,20},{5,21},{6,22},{7,23},{8,24},{9,... | collective-permute-start | bytes 589832 | tf_op jit(solution)/shard_map/ppermute | solution.py:43
  16.9 3.3 %collective-permute-start.2 = (bf16[2,16,3072]{2,1,0:T(8,128)(2,1)S(1)}, bf16[2,16,3072]{2,1,0:T(8,128)(2,1)S(1)}, u32[]{:S(2)}, u32[]{:S(2)}) collective-permute-start(bf16[2,16,3072]{2,1,0:T(8,128)(2,1)S(1)} %get-tuple-element.27), channel_id=1, source_target_pairs={{0,32},{1,33},{2,34},{3,35},{4,36},{5,37},{6,38},{7,39},{8,40},{9,... | collective-permute-start | bytes 589832 | tf_op jit(solution)/shard_map/ppermute | solution.py:43
  20.2 1.2 %collective-permute-done.7.refs_1_ = bf16[128,3072]{1,0:T(8,128)(2,1)S(1)} collective-permute-done((bf16[128,3072]{1,0:T(8,128)(2,1)}, bf16[128,3072]{1,0:T(8,128)(2,1)S(1)}, u32[]{:S(2)}, u32[]{:S(2)}) %collective-permute-start.7) | collective-permute-done | bytes 786464 | tf_op jit(solution)/shard_map/ppermute | solution.py:43
  21.4 3.8 %collective-permute-start.3 = (bf16[2,16,3072]{2,1,0:T(8,128)(2,1)S(1)}, bf16[2,16,3072]{2,1,0:T(8,128)(2,1)S(1)}, u32[]{:S(2)}, u32[]{:S(2)}) collective-permute-start(bf16[2,16,3072]{2,1,0:T(8,128)(2,1)S(1)} %get-tuple-element.28), channel_id=1, source_target_pairs={{0,48},{1,49},{2,50},{3,51},{4,52},{5,53},{6,54},{7,55},{8,56},{9,... | collective-permute-start | bytes 589832 | tf_op jit(solution)/shard_map/ppermute | solution.py:43
  25.3 0.0 collective-permute-done.6.refs_0_
  25.3 0.5 relay.1
  25.8 2.8 %collective-permute-start.11 = (bf16[128,3072]{1,0:T(8,128)(2,1)S(1)}, bf16[128,3072]{1,0:T(8,128)(2,1)S(1)}, u32[]{:S(2)}, u32[]{:S(2)}) collective-permute-start(bf16[128,3072]{1,0:T(8,128)(2,1)S(1)} %get-tuple-element.31.refs_2_), channel_id=1, source_target_pairs={{0,6},{1,7},{2,0},{3,1},{4,2},{5,3},{6,4},{7,5},{8,14},{9,15},{10,... | collective-permute-start | bytes 2359304 | tf_op jit(solution)/shard_map/ppermute | solution.py:43
  28.6 0.0 collective-permute-done.1.refs_1_
  28.6 1.2 %collective-permute-start.9 = (bf16[128,3072]{1,0:T(8,128)(2,1)S(1)}, bf16[128,3072]{1,0:T(8,128)(2,1)S(1)}, u32[]{:S(2)}, u32[]{:S(2)}) collective-permute-start(bf16[128,3072]{1,0:T(8,128)(2,1)S(1)} %get-tuple-element.31.refs_2_), channel_id=1, source_target_pairs={{0,1},{1,0},{2,3},{3,2},{4,5},{5,4},{6,7},{7,6},{8,9},{9,8},{10,11... | collective-permute-start | bytes 2359304 | tf_op jit(solution)/shard_map/ppermute | solution.py:43
  29.9 0.0 collective-permute-done.2.refs_2_
  29.9 0.0 collective-permute-start.10
  29.9 0.0 collective-permute-done.3.refs_3_
  29.9 0.6 z_sums.1
  30.5 2.7 %collective-permute-start.4 = (f32[16,3072]{1,0:T(8,128)S(1)}, f32[16,3072]{1,0:T(8,128)S(1)}, u32[]{:S(2)}, u32[]{:S(2)}) collective-permute-start(f32[16,3072]{1,0:T(8,128)S(1)} %get-tuple-element.30), channel_id=1, source_target_pairs={{0,64},{1,65},{2,66},{3,67},{4,68},{5,69},{6,70},{7,71},{8,72},{9,... | collective-permute-start | bytes 589832 | tf_op jit(solution)/shard_map/ppermute | solution.py:43
  33.2 6.5 %hidden_grad_0.1 = (bf16[512,3072]{1,0:T(8,128)(2,1)S(1)}, bf16[8,128,1536]{2,1,0:T(8,128)(2,1)}) custom-call(s32[12]{0:T(128)S(1)} %dynamic-slice_bitcast_fusion.place, bf16[128,3072]{1,0:T(8,128)(2,1)S(1)} %bitcast.24, bf16[128,3072]{1,0:T(8,128)(2,1)S(1)} %collective-permute-done.5.refs_1_, bf16[128,3072]{1,0:T(8,128)(2,1)S(1)} %get-tuple-element.31.refs_2_, ...), custom_call_target="tpu_custom_call" | custom-call | flops 6700000256 | tf_op jit(solution)/shard_map/hidden_grad_0/pallas_call | solution.py:69
  39.7 5.6 %weight_grad_first.1 = (bf16[1536,3072]{1,0:T(8,128)(2,1)S(1)}, f32[8,128]{1,0:T(8,128)S(1)}) custom-call(s32[12]{0:T(128)S(1)} %dynamic-slice_bitcast_fusion.place, bf16[512,3072]{1,0:T(8,128)(2,1)S(1)} %get-tuple-element.33.refs_0_, bf16[1536,512]{1,0:T(8,128)(2,1)S(1)} %get-tuple-element.34.refs_1_), custom_call_target="tpu_custom_call" | custom-call | flops 5600000000 | tf_op jit(solution)/shard_map/weight_grad_first/pallas_call | solution.py:69
  45.4 3.9 %gelu_4.1 = (bf16[1536,512]{1,0:T(8,128)(2,1)S(1)}, f32[512,1536]{1,0:T(8,128)S(1)}) custom-call(s32[12]{0:T(128)S(1)} %dynamic-slice_bitcast_fusion.place, bf16[8,128,1536]{2,1,0:T(8,128)(2,1)} %bitcast.29, f32[8,128]{1,0:T(8,128)S(1)} %get-tuple-element.35.refs_1_), custom_call_target="tpu_custom_call" | custom-call | flops 2800000000 | tf_op jit(solution)/shard_map/gelu_4/pallas_call | solution.py:69
  49.2 0.0 copy-start
  49.2 0.0 copy-start.1
  49.3 0.0 collective-permute-done.9.refs_0_.refs_1_
  49.3 0.6 pick.1
  49.9 2.7 %collective-permute-start.15 = (bf16[128,3072]{1,0:T(8,128)(2,1)S(1)}, bf16[128,3072]{1,0:T(8,128)(2,1)S(1)}, u32[]{:S(2)}, u32[]{:S(2)}) collective-permute-start(bf16[128,3072]{1,0:T(8,128)(2,1)S(1)} %pick.1), channel_id=1, source_target_pairs={{0,2},{1,3},{2,4},{3,5},{4,6},{5,7},{6,0},{7,1},{8,14},{9,15},{10,... | collective-permute-start | bytes 2359304 | tf_op jit(solution)/shard_map/ppermute | solution.py:43
  52.6 0.0 collective-permute-done.4.refs_1_
  52.7 1.3 %outer_step.1 = (f32[16,3072]{1,0:T(8,128)}, bf16[16,3072]{1,0:T(8,128)(2,1)S(1)}) custom-call(s32[12]{0:T(128)S(1)} %dynamic-slice_bitcast_fusion.place, f32[16,3072]{1,0:T(8,128)S(1)} %get-tuple-element.29.refs_6_.refs_0_, f32[16,3072]{1,0:T(8,128)S(1)} %collective-permute-done.4.refs_1_, bf16[16,16,3072]{2,1,0:T(8,128)(2,1)S(1)} %bitcast.19, ...), custom_call_target="tpu_custom_call" | custom-call | flops 700000000 | tf_op jit(solution)/shard_map/outer_step/pallas_call | solution.py:69
  53.9 0.5 collective-permute-start.8
  54.5 0.0 collective-permute-done.11.refs_2_
  54.5 5.2 %hidden_grad_4.1 = (bf16[384,3072]{1,0:T(8,128)(2,1)S(1)}, bf16[8,128,1536]{2,1,0:T(8,128)(2,1)}) custom-call(s32[12]{0:T(128)S(1)} %dynamic-slice_bitcast_fusion.place, bf16[128,3072]{1,0:T(8,128)(2,1)S(1)} %collective-permute-done.9.refs_0_.refs_1_, bf16[128,3072]{1,0:T(8,128)(2,1)S(1)} %collective-permute-done.10.refs_1_.refs_0_, ...), custom_call_target="tpu_custom_call", output_to_operand_aliasing={{1}: (6, {})} | custom-call | flops 5400000000 | tf_op jit(solution)/shard_map/hidden_grad_4/pallas_call | solution.py:69
  59.7 0.0 collective-permute-done.8.refs_1_
  59.7 0.6 stack.2.refs_4_.refs_0_
  60.3 1.0 %collective-permute-start.14 = (bf16[2,16,3072]{2,1,0:T(8,128)(2,1)S(1)}, bf16[2,16,3072]{2,1,0:T(8,128)(2,1)S(1)}, u32[]{:S(2)}, u32[]{:S(2)}) collective-permute-start(bf16[2,16,3072]{2,1,0:T(8,128)(2,1)S(1)} %stack.2.refs_4_.refs_0_), channel_id=1, source_target_pairs={{0,16},{1,17},{2,18},{3,19},{4,20},{5,21},{6,22},{7,23},{8,24},{9,... | collective-permute-start | bytes 589832 | tf_op jit(solution)/shard_map/ppermute | solution.py:43
  61.3 2.4 %collective-permute-start.13 = (bf16[2,16,3072]{2,1,0:T(8,128)(2,1)S(1)}, bf16[2,16,3072]{2,1,0:T(8,128)(2,1)S(1)}, u32[]{:S(2)}, u32[]{:S(2)}) collective-permute-start(bf16[2,16,3072]{2,1,0:T(8,128)(2,1)S(1)} %stack.2.refs_4_.refs_0_), channel_id=1, source_target_pairs={{0,32},{1,33},{2,34},{3,35},{4,36},{5,37},{6,38},{7,39},{8,40},{9,... | collective-permute-start | bytes 589832 | tf_op jit(solution)/shard_map/ppermute | solution.py:43
  63.7 0.1 collective-permute-start.12
  63.8 0.0 collective-permute-done.15.refs_0_.refs_1_
  63.8 3.9 %hidden_grad_7.1.refs_4_ = bf16[8,128,1536]{2,1,0:T(8,128)(2,1)} custom-call(s32[12]{0:T(128)S(1)} %dynamic-slice_bitcast_fusion.place, bf16[128,3072]{1,0:T(8,128)(2,1)S(1)} %collective-permute-done.15.refs_0_.refs_1_, bf16[1536,3072]{1,0:T(8,128)(2,1)S(1)} %bitcast.17, ...), custom_call_target="tpu_custom_call", output_to_operand_aliasing={{}: (4, {})} | custom-call | flops 2800000000 | tf_op jit(solution)/shard_map/hidden_grad_7/pallas_call | solution.py:69
  67.7 0.0 collective-permute-done.14.refs_3_
  67.7 2.9 %collective-permute-done.13.refs_2_ = bf16[2,16,3072]{2,1,0:T(8,128)(2,1)S(1)} collective-permute-done((bf16[2,16,3072]{2,1,0:T(8,128)(2,1)S(1)}, bf16[2,16,3072]{2,1,0:T(8,128)(2,1)S(1)}, u32[]{:S(2)}, u32[]{:S(2)}) %collective-permute-start.13) | collective-permute-done | bytes 196640 | tf_op jit(solution)/shard_map/ppermute | solution.py:43
  70.6 0.6 stack.3.refs_4_.refs_0_
  71.2 3.2 %collective-permute-start.16 = (bf16[4,2,16,3072]{3,2,1,0:T(8,128)(2,1)S(1)}, bf16[4,2,16,3072]{3,2,1,0:T(8,128)(2,1)S(1)}, u32[]{:S(2)}, u32[]{:S(2)}) collective-permute-start(bf16[4,2,16,3072]{3,2,1,0:T(8,128)(2,1)S(1)} %stack.3.refs_4_.refs_0_), channel_id=1, source_target_pairs={{0,8},{1,9},{2,10},{3,11},{4,12},{5,13},{6,14},{7,15},{8,0},{9,1},... | collective-permute-start | bytes 2359304 | tf_op jit(solution)/shard_map/ppermute | solution.py:43
  74.5 7.5 %weight_grad_last.1.refs_2_ = bf16[1536,3072]{1,0:T(8,128)(2,1)} custom-call(s32[12]{0:T(128)S(1)} %dynamic-slice_bitcast_fusion.place, bf16[384,3072]{1,0:T(8,128)(2,1)S(1)} %get-tuple-element.39.refs_2_.refs_0_, bf16[128,3072]{1,0:T(8,128)(2,1)S(1)} %collective-permute-done.15.refs_0_.refs_1_, bf16[1536,512]{1,0:T(8,128)(2,1)S(1)} %get-tuple-element.41.refs_2_, ...), custom_call_target="tpu_custom_call" | custom-call | flops 8000000000 | tf_op jit(solution)/shard_map/weight_grad_last/pallas_call | solution.py:69
  82.0 1.8 %place_rows.1 = bf16[2,4,32,3072]{3,2,1,0:T(8,128)(2,1)} custom-call(s32[12]{0:T(128)S(1)} %dynamic-slice_bitcast_fusion.place, bf16[4,2,16,3072]{3,2,1,0:T(8,128)(2,1)S(1)} %stack.3.refs_4_.refs_0_, bf16[4,2,16,3072]{3,2,1,0:T(8,128)(2,1)S(1)} %collective-permute-done.16.refs_1_, bf16[1536,3072]{1,0:T(8,128)(2,1)} %weight_grad_last.1.refs_2_), custom_call_target="tpu_custom_call" | custom-call | flops 1500000000 | tf_op jit(solution)/shard_map/place_rows/pallas_call | solution.py:69
  (15 shorter events, 0.0 us)
Async XLA Ops:
  0.6 11.0 %collective-permute-start = (bf16[2,4,32,3072]{3,2,1,0:T(8,128)(2,1)}, bf16[2,4,32,3072]{3,2,1,0:T(8,128)(2,1)}, u32[]{:S(2)}, u32[]{:S(2)}) collective-permute-start(bf16[2,4,32,3072]{3,2,1,0:T(8,128)(2,1)} %bitcast.30), channel_id=1, source_target_pairs={{0,8},{1,9},{2,10},{3,11},{4,12},{5,13},{6,14},{7,15},{8,0},{9,1},... | collective-permute-start | bytes 4718600 | tf_op jit(solution)/shard_map/ppermute | solution.py:43
  2.1 19.3 %collective-permute-start.7 = (bf16[128,3072]{1,0:T(8,128)(2,1)}, bf16[128,3072]{1,0:T(8,128)(2,1)S(1)}, u32[]{:S(2)}, u32[]{:S(2)}) collective-permute-start(bf16[128,3072]{1,0:T(8,128)(2,1)} %bitcast.21), channel_id=1, source_target_pairs={{0,1},{1,0},{2,3},{3,2},{4,5},{5,4},{6,7},{7,6},{8,9},{9,8},{10,11... | collective-permute-start | bytes 2359304 | tf_op jit(solution)/shard_map/ppermute | solution.py:43
  3.4 21.8 %collective-permute-start.6 = (bf16[128,3072]{1,0:T(8,128)(2,1)}, bf16[128,3072]{1,0:T(8,128)(2,1)S(1)}, u32[]{:S(2)}, u32[]{:S(2)}) collective-permute-start(bf16[128,3072]{1,0:T(8,128)(2,1)} %bitcast.22), channel_id=1, source_target_pairs={{0,6},{1,7},{2,0},{3,1},{4,2},{5,3},{6,4},{7,5},{8,14},{9,15},{10,... | collective-permute-start | bytes 2359304 | tf_op jit(solution)/shard_map/ppermute | solution.py:43
  6.2 27.0 %collective-permute-start.5 = (bf16[128,3072]{1,0:T(8,128)(2,1)}, bf16[128,3072]{1,0:T(8,128)(2,1)S(1)}, u32[]{:S(2)}, u32[]{:S(2)}) collective-permute-start(bf16[128,3072]{1,0:T(8,128)(2,1)} %bitcast.23), channel_id=1, source_target_pairs={{0,2},{1,3},{2,4},{3,5},{4,6},{5,7},{6,0},{7,1},{8,10},{9,11},{10,... | collective-permute-start | bytes 2359304 | tf_op jit(solution)/shard_map/ppermute | solution.py:43
  6.9 26.3 %slice-start = ((s8[9437184]{0:T(1024)(128)(4,1)}), s8[4194304]{0:T(1024)(128)(4,1)S(1)}, s32[]{:S(2)}) async-start(s8[9437184]{0:T(1024)(128)(4,1)} %bitcast.13), calls=%async_computation | async-start | bytes 8388608
  6.9 26.3 %slice-start.1 = ((s8[9437184]{0:T(1024)(128)(4,1)}), s8[4194304]{0:T(1024)(128)(4,1)S(1)}, s32[]{:S(2)}) async-start(s8[9437184]{0:T(1024)(128)(4,1)} %bitcast.13), calls=%async_computation.1 | async-start | bytes 8388608
  11.6 21.6 %slice-start.2 = ((s8[9437184]{0:T(1024)(128)(4,1)}), s8[1048576]{0:T(1024)(128)(4,1)S(1)}, s32[]{:S(2)}) async-start(s8[9437184]{0:T(1024)(128)(4,1)} %bitcast.13), calls=%async_computation.2 | async-start | bytes 2097152
  15.2 18.1 %copy-start.2 = (bf16[1,128,3072]{2,1,0:T(8,128)(2,1)S(1)}, bf16[1,128,3072]{2,1,0:T(8,128)(2,1)}, u32[]{:S(2)}) copy-start(bf16[1,128,3072]{2,1,0:T(8,128)(2,1)} %param.10) | copy-start | bytes 2359300
  15.2 13.5 %collective-permute-start.1 = (bf16[2,16,3072]{2,1,0:T(8,128)(2,1)S(1)}, bf16[2,16,3072]{2,1,0:T(8,128)(2,1)S(1)}, u32[]{:S(2)}, u32[]{:S(2)}) collective-permute-start(bf16[2,16,3072]{2,1,0:T(8,128)(2,1)S(1)} %get-tuple-element.26), channel_id=1, source_target_pairs={{0,16},{1,17},{2,18},{3,19},{4,20},{5,21},{6,22},{7,23},{8,24},{9,... | collective-permute-start | bytes 589832 | tf_op jit(solution)/shard_map/ppermute | solution.py:43
  16.9 13.0 %collective-permute-start.2 = (bf16[2,16,3072]{2,1,0:T(8,128)(2,1)S(1)}, bf16[2,16,3072]{2,1,0:T(8,128)(2,1)S(1)}, u32[]{:S(2)}, u32[]{:S(2)}) collective-permute-start(bf16[2,16,3072]{2,1,0:T(8,128)(2,1)S(1)} %get-tuple-element.27), channel_id=1, source_target_pairs={{0,32},{1,33},{2,34},{3,35},{4,36},{5,37},{6,38},{7,39},{8,40},{9,... | collective-permute-start | bytes 589832 | tf_op jit(solution)/shard_map/ppermute | solution.py:43
  21.4 8.4 %collective-permute-start.3 = (bf16[2,16,3072]{2,1,0:T(8,128)(2,1)S(1)}, bf16[2,16,3072]{2,1,0:T(8,128)(2,1)S(1)}, u32[]{:S(2)}, u32[]{:S(2)}) collective-permute-start(bf16[2,16,3072]{2,1,0:T(8,128)(2,1)S(1)} %get-tuple-element.28), channel_id=1, source_target_pairs={{0,48},{1,49},{2,50},{3,51},{4,52},{5,53},{6,54},{7,55},{8,56},{9,... | collective-permute-start | bytes 589832 | tf_op jit(solution)/shard_map/ppermute | solution.py:43
  25.8 28.6 %collective-permute-start.11 = (bf16[128,3072]{1,0:T(8,128)(2,1)S(1)}, bf16[128,3072]{1,0:T(8,128)(2,1)S(1)}, u32[]{:S(2)}, u32[]{:S(2)}) collective-permute-start(bf16[128,3072]{1,0:T(8,128)(2,1)S(1)} %get-tuple-element.31.refs_2_), channel_id=1, source_target_pairs={{0,6},{1,7},{2,0},{3,1},{4,2},{5,3},{6,4},{7,5},{8,14},{9,15},{10,... | collective-permute-start | bytes 2359304 | tf_op jit(solution)/shard_map/ppermute | solution.py:43
  28.6 20.6 %collective-permute-start.9 = (bf16[128,3072]{1,0:T(8,128)(2,1)S(1)}, bf16[128,3072]{1,0:T(8,128)(2,1)S(1)}, u32[]{:S(2)}, u32[]{:S(2)}) collective-permute-start(bf16[128,3072]{1,0:T(8,128)(2,1)S(1)} %get-tuple-element.31.refs_2_), channel_id=1, source_target_pairs={{0,1},{1,0},{2,3},{3,2},{4,5},{5,4},{6,7},{7,6},{8,9},{9,8},{10,11... | collective-permute-start | bytes 2359304 | tf_op jit(solution)/shard_map/ppermute | solution.py:43
  29.9 19.4 %collective-permute-start.10 = (bf16[128,3072]{1,0:T(8,128)(2,1)S(1)}, bf16[128,3072]{1,0:T(8,128)(2,1)S(1)}, u32[]{:S(2)}, u32[]{:S(2)}) collective-permute-start(bf16[128,3072]{1,0:T(8,128)(2,1)S(1)} %get-tuple-element.32.refs_3_), channel_id=1, source_target_pairs={{0,2},{1,3},{2,4},{3,5},{4,6},{5,7},{6,0},{7,1},{8,10},{9,11},{10,... | collective-permute-start | bytes 2359304 | tf_op jit(solution)/shard_map/ppermute | solution.py:43
  30.5 22.2 %collective-permute-start.4 = (f32[16,3072]{1,0:T(8,128)S(1)}, f32[16,3072]{1,0:T(8,128)S(1)}, u32[]{:S(2)}, u32[]{:S(2)}) collective-permute-start(f32[16,3072]{1,0:T(8,128)S(1)} %get-tuple-element.30), channel_id=1, source_target_pairs={{0,64},{1,65},{2,66},{3,67},{4,68},{5,69},{6,70},{7,71},{8,72},{9,... | collective-permute-start | bytes 589832 | tf_op jit(solution)/shard_map/ppermute | solution.py:43
  49.2 3.4 %copy-start = (bf16[1,256,3072]{2,1,0:T(8,128)(2,1)S(1)}, bf16[1,256,3072]{2,1,0:T(8,128)(2,1)}, u32[]{:S(2)}) copy-start(bf16[1,256,3072]{2,1,0:T(8,128)(2,1)} %param.7) | copy-start | bytes 4718596
  49.2 3.4 %copy-start.1 = (f32[1,16,3072]{2,1,0:T(8,128)S(1)}, f32[1,16,3072]{2,1,0:T(8,128)}, u32[]{:S(2)}) copy-start(f32[1,16,3072]{2,1,0:T(8,128)} %param.9) | copy-start | bytes 589828
  49.9 13.9 %collective-permute-start.15 = (bf16[128,3072]{1,0:T(8,128)(2,1)S(1)}, bf16[128,3072]{1,0:T(8,128)(2,1)S(1)}, u32[]{:S(2)}, u32[]{:S(2)}) collective-permute-start(bf16[128,3072]{1,0:T(8,128)(2,1)S(1)} %pick.1), channel_id=1, source_target_pairs={{0,2},{1,3},{2,4},{3,5},{4,6},{5,7},{6,0},{7,1},{8,14},{9,15},{10,... | collective-permute-start | bytes 2359304 | tf_op jit(solution)/shard_map/ppermute | solution.py:43
  53.9 5.8 %collective-permute-start.8 = (bf16[16,3072]{1,0:T(8,128)(2,1)S(1)}, bf16[16,3072]{1,0:T(8,128)(2,1)S(1)}, u32[]{:S(2)}, u32[]{:S(2)}) collective-permute-start(bf16[16,3072]{1,0:T(8,128)(2,1)S(1)} %get-tuple-element.37.refs_6_.refs_0_), channel_id=1, source_target_pairs={{0,64},{1,65},{2,66},{3,67},{4,68},{5,69},{6,70},{7,71},{8,72},{9,... | collective-permute-start | bytes 294920 | tf_op jit(solution)/shard_map/ppermute | solution.py:43
  60.3 7.5 %collective-permute-start.14 = (bf16[2,16,3072]{2,1,0:T(8,128)(2,1)S(1)}, bf16[2,16,3072]{2,1,0:T(8,128)(2,1)S(1)}, u32[]{:S(2)}, u32[]{:S(2)}) collective-permute-start(bf16[2,16,3072]{2,1,0:T(8,128)(2,1)S(1)} %stack.2.refs_4_.refs_0_), channel_id=1, source_target_pairs={{0,16},{1,17},{2,18},{3,19},{4,20},{5,21},{6,22},{7,23},{8,24},{9,... | collective-permute-start | bytes 589832 | tf_op jit(solution)/shard_map/ppermute | solution.py:43
  61.3 9.3 %collective-permute-start.13 = (bf16[2,16,3072]{2,1,0:T(8,128)(2,1)S(1)}, bf16[2,16,3072]{2,1,0:T(8,128)(2,1)S(1)}, u32[]{:S(2)}, u32[]{:S(2)}) collective-permute-start(bf16[2,16,3072]{2,1,0:T(8,128)(2,1)S(1)} %stack.2.refs_4_.refs_0_), channel_id=1, source_target_pairs={{0,32},{1,33},{2,34},{3,35},{4,36},{5,37},{6,38},{7,39},{8,40},{9,... | collective-permute-start | bytes 589832 | tf_op jit(solution)/shard_map/ppermute | solution.py:43
  63.7 6.9 %collective-permute-start.12 = (bf16[2,16,3072]{2,1,0:T(8,128)(2,1)S(1)}, bf16[2,16,3072]{2,1,0:T(8,128)(2,1)S(1)}, u32[]{:S(2)}, u32[]{:S(2)}) collective-permute-start(bf16[2,16,3072]{2,1,0:T(8,128)(2,1)S(1)} %stack.2.refs_4_.refs_0_), channel_id=1, source_target_pairs={{0,48},{1,49},{2,50},{3,51},{4,52},{5,53},{6,54},{7,55},{8,56},{9,... | collective-permute-start | bytes 589832 | tf_op jit(solution)/shard_map/ppermute | solution.py:43
  71.2 10.8 %collective-permute-start.16 = (bf16[4,2,16,3072]{3,2,1,0:T(8,128)(2,1)S(1)}, bf16[4,2,16,3072]{3,2,1,0:T(8,128)(2,1)S(1)}, u32[]{:S(2)}, u32[]{:S(2)}) collective-permute-start(bf16[4,2,16,3072]{3,2,1,0:T(8,128)(2,1)S(1)} %stack.3.refs_4_.refs_0_), channel_id=1, source_target_pairs={{0,8},{1,9},{2,10},{3,11},{4,12},{5,13},{6,14},{7,15},{8,0},{9,1},... | collective-permute-start | bytes 2359304 | tf_op jit(solution)/shard_map/ppermute | solution.py:43

commit v4 on v2

--- a/solution.py
+++ b/solution.py
@@ -264,25 +264,31 @@
         partial[:, cols] = jnp.dot(hidden_t[...], rows[:, cols], preferred_element_type=jnp.float32).astype(jnp.bfloat16)
 
 
-TALL = 512
-
-
-def weight_grad_last(place, most, chunk, hidden_t, partial, weight_grad, rows, block, sems):
-    join((most, chunk), rows)
+TALL = 384
+
+
+def weight_grad_rows(first, rows, hidden_t, partial, weight_grad, block, sems):
     stored = []
-    for i in range(FF // TALL):
-        here = slice(i * TALL, (i + 1) * TALL)
-        if i >= 2:
-            stored[i - 2].wait()
+    for i in range(2):
+        here = slice(first + i * TALL, first + (i + 1) * TALL)
         for j in range(D // WIDE):
             cols = slice(j * WIDE, (j + 1) * WIDE)
             total = jnp.dot(hidden_t[here], rows[:, cols], preferred_element_type=jnp.float32)
-            block[i % 2, :, cols] = (partial[here, cols].astype(jnp.float32) + total).astype(jnp.bfloat16)
-        store = pltpu.make_async_copy(block.at[i % 2], weight_grad.at[here], sems.at[i % 2])
+            block[i, :, cols] = (partial[here, cols].astype(jnp.float32) + total).astype(jnp.bfloat16)
+        store = pltpu.make_async_copy(block.at[i], weight_grad.at[here], sems.at[i])
         store.start()
         stored.append(store)
-    for store in stored[-2:]:
+    for store in stored:
         store.wait()
+
+
+def weight_grad_upper(place, most, chunk, hidden_t, partial, rows, weight_grad, block, sems):
+    join((most, chunk), rows)
+    weight_grad_rows(0, rows, hidden_t, partial, weight_grad, block, sems)
+
+
+def weight_grad_lower(place, rows, hidden_t, partial, _, weight_grad, block, sems):
+    weight_grad_rows(2 * TALL, rows, hidden_t, partial, weight_grad, block, sems)
 
 
 def shards(anchor, local_params, momentum, out_grad, pre_act, down_weight):
@@ -345,7 +351,7 @@
         (VMEM,) * 2,
         aliases={1: 0, 2: 1},
         us=0.1,
-        after=[mine],
+        after=[kept],
     )
     rows_0, pre_grad = run_hidden_grad(place, 0, [own, ym, yp, x], w, slope_0, after=[mine])
     xyp = shift(yp, xl=1)
@@ -377,7 +383,7 @@
     passed = call(
         pick, place, [xym, xyp], [VMEM] * 2, pltpu.VMEM((CHUNK, D), bf16), VMEM, us=0.4, after=[slope_4]
     )
-    x2 = shift(passed, y=lambda c: 1 - 2 * c)
+    x2 = shift(passed, y=lambda core: 1 - 2 * core)
     new_momentum, rows = call(
         outer_step,
         place,
@@ -396,18 +402,31 @@
     )
     pairs = [pair, shift(pair, z=3), shift(pair, z=2), shift(pair, z=1)]
     (pre_grad,) = run_hidden_grad(place, 7, [x2], w, slope_4, pre_grad, after=[pair])
-    mine = call(stack, place, pairs, [VMEM] * 4, pltpu.VMEM((4, 2, ROWS, D), bf16), VMEM, us=0.8, after=[pre_grad])
+    rows_4, upper = call(
+        weight_grad_upper,
+        place,
+        [rows_4, x2, ht_4, partial],
+        [VMEM] * 4,
+        (pltpu.VMEM((4 * CHUNK, D), bf16), pltpu.HBM((FF, D), bf16)),
+        (VMEM, HBM),
+        [pltpu.VMEM((2, TALL, D), bf16), pltpu.SemaphoreType.DMA((2,))],
+        limit=12,
+        us=4.5,
+        after=[pre_grad],
+    )
+    mine = call(stack, place, pairs, [VMEM] * 4, pltpu.VMEM((4, 2, ROWS, D), bf16), VMEM, us=0.8, after=[upper])
     other = shift(mine, c=1)
     weight_grad = call(
-        weight_grad_last,
-        place,
-        [rows_4, x2, ht_4, partial],
-        [VMEM] * 4,
+        weight_grad_lower,
+        place,
+        [rows_4, ht_4, partial, upper],
+        [VMEM] * 3 + [HBM],
         pltpu.HBM((FF, D), bf16),
         HBM,
-        [pltpu.VMEM((4 * CHUNK, D), bf16), pltpu.VMEM((2, TALL, D), bf16), pltpu.SemaphoreType.DMA((2,))],
-        limit=13,
-        us=8.0,
+        [pltpu.VMEM((2, TALL, D), bf16), pltpu.SemaphoreType.DMA((2,))],
+        limit=12,
+        aliases={4: 0},
+        us=4.5,
         after=[mine],
     )
     new_anchor = call(

time: 86 us -> 83.2 us (0.967)
  waiting for transfers between devices: 8.95 us -> 1.93 us
  starting transfers between devices: 28.8 us -> 31.3 us
  Pallas kernels: 46.4 us -> 48 us
    ppermute x17, waiting for transfers between devices: 8.95 us -> 1.93 us  [shift(): return lax.ppermute(array, AXES, pairs)]
    ppermute x17, starting transfers between devices: 28.8 us -> 31.3 us  [shift(): return lax.ppermute(array, AXES, pairs)]
    pallas_call x15 -> x16, Pallas kernels: 46.4 us -> 48 us  [call(): pl.pallas_call(body, out_shape=out_shape, in_specs=[SMEM, *in_specs, *aft...]
  transfers between devices with their start and end apart: 17 -> 17, of which waited for: 4 -> 1; matrix products, arithmetic and copies ran while one was open for 1% -> 1% of each run, Pallas kernels for 51% -> 55%
where the time goes in v4:
time: 83.2 us; the launch traced here: 83.1 us
  Pallas kernels  48 us (58%)
  starting transfers between devices  31.3 us (38%)
  waiting for transfers between devices  1.93 us (2%)
  between operations  1.07 us (1%)
    pallas_call x16, Pallas kernels, call(): pl.pallas_call(body, out_shape=out_shape, in_specs=[SMEM, *in_specs, *aft...  48 us
    ppermute x17, starting transfers between devices, shift(): return lax.ppermute(array, AXES, pairs)  31.3 us
    ppermute x17, waiting for transfers between devices, shift(): return lax.ppermute(array, AXES, pairs)  1.93 us
  transfers between devices with their start and end apart: 17, of which 1 were waited for; matrix products, arithmetic and copies ran while one was open for 1% of the time, Pallas kernels for 55%

profile of v4, /device:TPU:1, one launch (start us, length us, event | category | flops | bytes accessed | tf_op | source)
XLA Modules:
  0.0 83.1 jit_solution(17720175656313013943)
XLA Ops:
  0.6 1.5 %collective-permute-start = (bf16[2,4,32,3072]{3,2,1,0:T(8,128)(2,1)}, bf16[2,4,32,3072]{3,2,1,0:T(8,128)(2,1)}, u32[]{:S(2)}, u32[]{:S(2)}) collective-permute-start(bf16[2,4,32,3072]{3,2,1,0:T(8,128)(2,1)} %bitcast.30), channel_id=1, source_target_pairs={{0,8},{1,9},{2,10},{3,11},{4,12},{5,13},{6,14},{7,15},{8,0},{9,1},... | collective-permute-start | bytes 4718600 | tf_op jit(solution)/shard_map/ppermute | solution.py:43
  2.1 1.3 %collective-permute-start.7 = (bf16[128,3072]{1,0:T(8,128)(2,1)}, bf16[128,3072]{1,0:T(8,128)(2,1)S(1)}, u32[]{:S(2)}, u32[]{:S(2)}) collective-permute-start(bf16[128,3072]{1,0:T(8,128)(2,1)} %bitcast.21), channel_id=1, source_target_pairs={{0,1},{1,0},{2,3},{3,2},{4,5},{5,4},{6,7},{7,6},{8,9},{9,8},{10,11... | collective-permute-start | bytes 2359304 | tf_op jit(solution)/shard_map/ppermute | solution.py:43
  3.4 2.7 %collective-permute-start.6 = (bf16[128,3072]{1,0:T(8,128)(2,1)}, bf16[128,3072]{1,0:T(8,128)(2,1)S(1)}, u32[]{:S(2)}, u32[]{:S(2)}) collective-permute-start(bf16[128,3072]{1,0:T(8,128)(2,1)} %bitcast.22), channel_id=1, source_target_pairs={{0,6},{1,7},{2,0},{3,1},{4,2},{5,3},{6,4},{7,5},{8,14},{9,15},{10,... | collective-permute-start | bytes 2359304 | tf_op jit(solution)/shard_map/ppermute | solution.py:43
  6.2 0.0 collective-permute-start.5
  6.2 0.7 dynamic-slice_bitcast_fusion.place
  6.9 4.1 %gelu_0.1 = (bf16[1536,512]{1,0:T(8,128)(2,1)S(1)}, f32[512,1536]{1,0:T(8,128)S(1)}) custom-call(s32[12]{0:T(128)S(1)} %dynamic-slice_bitcast_fusion.place, bf16[8,128,1536]{2,1,0:T(8,128)(2,1)} %bitcast.28), custom_call_target="tpu_custom_call" | custom-call | flops 2800000000 | tf_op jit(solution)/shard_map/gelu_0/pallas_call | solution.py:69
  11.0 0.0 collective-permute-done.refs_2_
  11.0 0.0 slice-start.2
  11.0 3.5 %drift_sums.1 = (f32[2,16,3072]{2,1,0:T(8,128)S(1)}, bf16[2,16,3072]{2,1,0:T(8,128)(2,1)S(1)}, bf16[2,16,3072]{2,1,0:T(8,128)(2,1)S(1)}, bf16[2,16,3072]{2,1,0:T(8,128)(2,1)S(1)}) custom-call(s32[12]{0:T(128)S(1)} %dynamic-slice_bitcast_fusion.place, bf16[2,4,32,3072]{3,2,1,0:T(8,128)(2,1)} %bitcast.18, bf16[2,4,32,3072]{3,2,1,0:T(8,128)(2,1)} %bitcast.31, ...), custom_call_target="tpu_custom_call" | custom-call | flops 3000000000 | tf_op jit(solution)/shard_map/drift_sums/pallas_call | solution.py:69
  14.5 0.0 copy-start.2
  14.5 1.7 %collective-permute-start.1 = (bf16[2,16,3072]{2,1,0:T(8,128)(2,1)S(1)}, bf16[2,16,3072]{2,1,0:T(8,128)(2,1)S(1)}, u32[]{:S(2)}, u32[]{:S(2)}) collective-permute-start(bf16[2,16,3072]{2,1,0:T(8,128)(2,1)S(1)} %get-tuple-element.28), channel_id=1, source_target_pairs={{0,16},{1,17},{2,18},{3,19},{4,20},{5,21},{6,22},{7,23},{8,24},{9,... | collective-permute-start | bytes 589832 | tf_op jit(solution)/shard_map/ppermute | solution.py:43
  16.3 3.3 %collective-permute-start.2 = (bf16[2,16,3072]{2,1,0:T(8,128)(2,1)S(1)}, bf16[2,16,3072]{2,1,0:T(8,128)(2,1)S(1)}, u32[]{:S(2)}, u32[]{:S(2)}) collective-permute-start(bf16[2,16,3072]{2,1,0:T(8,128)(2,1)S(1)} %get-tuple-element.29), channel_id=1, source_target_pairs={{0,32},{1,33},{2,34},{3,35},{4,36},{5,37},{6,38},{7,39},{8,40},{9,... | collective-permute-start | bytes 589832 | tf_op jit(solution)/shard_map/ppermute | solution.py:43
  19.6 1.9 %collective-permute-done.7.refs_1_ = bf16[128,3072]{1,0:T(8,128)(2,1)S(1)} collective-permute-done((bf16[128,3072]{1,0:T(8,128)(2,1)}, bf16[128,3072]{1,0:T(8,128)(2,1)S(1)}, u32[]{:S(2)}, u32[]{:S(2)}) %collective-permute-start.7) | collective-permute-done | bytes 786464 | tf_op jit(solution)/shard_map/ppermute | solution.py:43
  21.4 3.8 %collective-permute-start.3 = (bf16[2,16,3072]{2,1,0:T(8,128)(2,1)S(1)}, bf16[2,16,3072]{2,1,0:T(8,128)(2,1)S(1)}, u32[]{:S(2)}, u32[]{:S(2)}) collective-permute-start(bf16[2,16,3072]{2,1,0:T(8,128)(2,1)S(1)} %get-tuple-element.30), channel_id=1, source_target_pairs={{0,48},{1,49},{2,50},{3,51},{4,52},{5,53},{6,54},{7,55},{8,56},{9,... | collective-permute-start | bytes 589832 | tf_op jit(solution)/shard_map/ppermute | solution.py:43
  25.3 0.0 collective-permute-done.6.refs_0_
  25.3 0.5 relay.1
  25.8 2.8 %collective-permute-start.11 = (bf16[128,3072]{1,0:T(8,128)(2,1)S(1)}, bf16[128,3072]{1,0:T(8,128)(2,1)S(1)}, u32[]{:S(2)}, u32[]{:S(2)}) collective-permute-start(bf16[128,3072]{1,0:T(8,128)(2,1)S(1)} %get-tuple-element.33.refs_2_), channel_id=1, source_target_pairs={{0,6},{1,7},{2,0},{3,1},{4,2},{5,3},{6,4},{7,5},{8,14},{9,15},{10,... | collective-permute-start | bytes 2359304 | tf_op jit(solution)/shard_map/ppermute | solution.py:43
  28.6 0.0 collective-permute-done.1.refs_1_
  28.6 1.2 %collective-permute-start.9 = (bf16[128,3072]{1,0:T(8,128)(2,1)S(1)}, bf16[128,3072]{1,0:T(8,128)(2,1)S(1)}, u32[]{:S(2)}, u32[]{:S(2)}) collective-permute-start(bf16[128,3072]{1,0:T(8,128)(2,1)S(1)} %get-tuple-element.33.refs_2_), channel_id=1, source_target_pairs={{0,1},{1,0},{2,3},{3,2},{4,5},{5,4},{6,7},{7,6},{8,9},{9,8},{10,11... | collective-permute-start | bytes 2359304 | tf_op jit(solution)/shard_map/ppermute | solution.py:43
  29.9 0.0 collective-permute-done.2.refs_2_
  29.9 0.0 collective-permute-start.10
  29.9 0.6 z_sums.1
  30.5 2.7 %collective-permute-start.4 = (f32[16,3072]{1,0:T(8,128)S(1)}, f32[16,3072]{1,0:T(8,128)S(1)}, u32[]{:S(2)}, u32[]{:S(2)}) collective-permute-start(f32[16,3072]{1,0:T(8,128)S(1)} %get-tuple-element.32), channel_id=1, source_target_pairs={{0,64},{1,65},{2,66},{3,67},{4,68},{5,69},{6,70},{7,71},{8,72},{9,... | collective-permute-start | bytes 589832 | tf_op jit(solution)/shard_map/ppermute | solution.py:43
  33.3 6.5 %hidden_grad_0.1 = (bf16[512,3072]{1,0:T(8,128)(2,1)S(1)}, bf16[8,128,1536]{2,1,0:T(8,128)(2,1)}) custom-call(s32[12]{0:T(128)S(1)} %dynamic-slice_bitcast_fusion.place, bf16[128,3072]{1,0:T(8,128)(2,1)S(1)} %bitcast.24, bf16[128,3072]{1,0:T(8,128)(2,1)S(1)} %collective-permute-done.5.refs_1_, bf16[128,3072]{1,0:T(8,128)(2,1)S(1)} %get-tuple-element.33.refs_2_, ...), custom_call_target="tpu_custom_call" | custom-call | flops 6700000256 | tf_op jit(solution)/shard_map/hidden_grad_0/pallas_call | solution.py:69
  39.8 5.7 %weight_grad_first.1 = (bf16[1536,3072]{1,0:T(8,128)(2,1)S(1)}, f32[8,128]{1,0:T(8,128)S(1)}) custom-call(s32[12]{0:T(128)S(1)} %dynamic-slice_bitcast_fusion.place, bf16[512,3072]{1,0:T(8,128)(2,1)S(1)} %get-tuple-element.35.refs_0_, bf16[1536,512]{1,0:T(8,128)(2,1)S(1)} %get-tuple-element.36.refs_1_), custom_call_target="tpu_custom_call" | custom-call | flops 5600000000 | tf_op jit(solution)/shard_map/weight_grad_first/pallas_call | solution.py:69
  45.5 3.8 %gelu_4.1 = (bf16[1536,512]{1,0:T(8,128)(2,1)S(1)}, f32[512,1536]{1,0:T(8,128)S(1)}) custom-call(s32[12]{0:T(128)S(1)} %dynamic-slice_bitcast_fusion.place, bf16[8,128,1536]{2,1,0:T(8,128)(2,1)} %bitcast.29, f32[8,128]{1,0:T(8,128)S(1)} %get-tuple-element.37.refs_1_), custom_call_target="tpu_custom_call" | custom-call | flops 2800000000 | tf_op jit(solution)/shard_map/gelu_4/pallas_call | solution.py:69
  49.4 0.0 copy-start
  49.4 0.0 copy-start.1
  49.4 0.0 collective-permute-done.10.refs_1_.refs_0_
  49.4 0.6 pick.1
  50.0 2.8 %collective-permute-start.15 = (bf16[128,3072]{1,0:T(8,128)(2,1)S(1)}, bf16[128,3072]{1,0:T(8,128)(2,1)S(1)}, u32[]{:S(2)}, u32[]{:S(2)}) collective-permute-start(bf16[128,3072]{1,0:T(8,128)(2,1)S(1)} %pick.1), channel_id=1, source_target_pairs={{0,2},{1,3},{2,4},{3,5},{4,6},{5,7},{6,0},{7,1},{8,14},{9,15},{10,... | collective-permute-start | bytes 2359304 | tf_op jit(solution)/shard_map/ppermute | solution.py:43
  52.8 0.0 collective-permute-done.4.refs_1_
  52.8 1.3 %outer_step.1 = (f32[16,3072]{1,0:T(8,128)}, bf16[16,3072]{1,0:T(8,128)(2,1)S(1)}) custom-call(s32[12]{0:T(128)S(1)} %dynamic-slice_bitcast_fusion.place, f32[16,3072]{1,0:T(8,128)S(1)} %get-tuple-element.31.refs_6_.refs_0_, f32[16,3072]{1,0:T(8,128)S(1)} %collective-permute-done.4.refs_1_, bf16[16,16,3072]{2,1,0:T(8,128)(2,1)S(1)} %bitcast.19, ...), custom_call_target="tpu_custom_call" | custom-call | flops 700000000 | tf_op jit(solution)/shard_map/outer_step/pallas_call | solution.py:69
  54.1 0.5 collective-permute-start.8
  54.6 0.0 collective-permute-done.11.refs_2_
  54.6 5.2 %hidden_grad_4.1 = (bf16[384,3072]{1,0:T(8,128)(2,1)S(1)}, bf16[8,128,1536]{2,1,0:T(8,128)(2,1)}) custom-call(s32[12]{0:T(128)S(1)} %dynamic-slice_bitcast_fusion.place, bf16[128,3072]{1,0:T(8,128)(2,1)S(1)} %collective-permute-done.9.refs_0_.refs_1_, bf16[128,3072]{1,0:T(8,128)(2,1)S(1)} %collective-permute-done.10.refs_1_.refs_0_, ...), custom_call_target="tpu_custom_call", output_to_operand_aliasing={{1}: (6, {})} | custom-call | flops 5400000000 | tf_op jit(solution)/shard_map/hidden_grad_4/pallas_call | solution.py:69
  59.8 0.6 stack.2.refs_4_.refs_0_
  60.4 0.1 collective-permute-start.14
  60.5 3.4 %collective-permute-start.13 = (bf16[2,16,3072]{2,1,0:T(8,128)(2,1)S(1)}, bf16[2,16,3072]{2,1,0:T(8,128)(2,1)S(1)}, u32[]{:S(2)}, u32[]{:S(2)}) collective-permute-start(bf16[2,16,3072]{2,1,0:T(8,128)(2,1)S(1)} %stack.2.refs_4_.refs_0_), channel_id=1, source_target_pairs={{0,32},{1,33},{2,34},{3,35},{4,36},{5,37},{6,38},{7,39},{8,40},{9,... | collective-permute-start | bytes 589832 | tf_op jit(solution)/shard_map/ppermute | solution.py:43
  63.9 3.9 %hidden_grad_7.1.refs_4_ = bf16[8,128,1536]{2,1,0:T(8,128)(2,1)} custom-call(s32[12]{0:T(128)S(1)} %dynamic-slice_bitcast_fusion.place, bf16[128,3072]{1,0:T(8,128)(2,1)S(1)} %collective-permute-done.15.refs_0_.refs_1_, bf16[1536,3072]{1,0:T(8,128)(2,1)S(1)} %bitcast.17, ...), custom_call_target="tpu_custom_call", output_to_operand_aliasing={{}: (4, {})} | custom-call | flops 2800000000 | tf_op jit(solution)/shard_map/hidden_grad_7/pallas_call | solution.py:69
  67.8 4.6 %weight_grad_upper.1 = (bf16[512,3072]{1,0:T(8,128)(2,1)S(1)}, bf16[1536,3072]{1,0:T(8,128)(2,1)}) custom-call(s32[12]{0:T(128)S(1)} %dynamic-slice_bitcast_fusion.place, bf16[384,3072]{1,0:T(8,128)(2,1)S(1)} %get-tuple-element.41.refs_2_.refs_0_, bf16[128,3072]{1,0:T(8,128)(2,1)S(1)} %collective-permute-done.15.refs_0_.refs_1_, ...), custom_call_target="tpu_custom_call" | custom-call | flops 4499999744 | tf_op jit(solution)/shard_map/weight_grad_upper/pallas_call | solution.py:69
  72.4 0.0 collective-permute-done.13.refs_2_
  72.4 0.0 collective-permute-done.12.refs_1_
  72.4 0.6 stack.3.refs_4_.refs_0_
  73.0 3.5 %collective-permute-start.16 = (bf16[4,2,16,3072]{3,2,1,0:T(8,128)(2,1)S(1)}, bf16[4,2,16,3072]{3,2,1,0:T(8,128)(2,1)S(1)}, u32[]{:S(2)}, u32[]{:S(2)}) collective-permute-start(bf16[4,2,16,3072]{3,2,1,0:T(8,128)(2,1)S(1)} %stack.3.refs_4_.refs_0_), channel_id=1, source_target_pairs={{0,8},{1,9},{2,10},{3,11},{4,12},{5,13},{6,14},{7,15},{8,0},{9,1},... | collective-permute-start | bytes 2359304 | tf_op jit(solution)/shard_map/ppermute | solution.py:43
  76.5 4.6 %weight_grad_lower.1.refs_2_ = bf16[1536,3072]{1,0:T(8,128)(2,1)} custom-call(s32[12]{0:T(128)S(1)} %dynamic-slice_bitcast_fusion.place, bf16[512,3072]{1,0:T(8,128)(2,1)S(1)} %get-tuple-element.46.refs_0_, bf16[1536,512]{1,0:T(8,128)(2,1)S(1)} %get-tuple-element.42.refs_2_.refs_1_, ...), custom_call_target="tpu_custom_call", output_to_operand_aliasing={{}: (4, {})} | custom-call | flops 4499999744 | tf_op jit(solution)/shard_map/weight_grad_lower/pallas_call | solution.py:69
  81.0 0.0 collective-permute-done.16.refs_1_
  81.1 1.8 %place_rows.1 = bf16[2,4,32,3072]{3,2,1,0:T(8,128)(2,1)} custom-call(s32[12]{0:T(128)S(1)} %dynamic-slice_bitcast_fusion.place, bf16[4,2,16,3072]{3,2,1,0:T(8,128)(2,1)S(1)} %stack.3.refs_4_.refs_0_, bf16[4,2,16,3072]{3,2,1,0:T(8,128)(2,1)S(1)} %collective-permute-done.16.refs_1_, bf16[1536,3072]{1,0:T(8,128)(2,1)} %weight_grad_lower.1.refs_2_), custom_call_target="tpu_custom_call" | custom-call | flops 1500000000 | tf_op jit(solution)/shard_map/place_rows/pallas_call | solution.py:69
  (16 shorter events, 0.0 us)
Async XLA Ops:
  0.6 10.4 %collective-permute-start = (bf16[2,4,32,3072]{3,2,1,0:T(8,128)(2,1)}, bf16[2,4,32,3072]{3,2,1,0:T(8,128)(2,1)}, u32[]{:S(2)}, u32[]{:S(2)}) collective-permute-start(bf16[2,4,32,3072]{3,2,1,0:T(8,128)(2,1)} %bitcast.30), channel_id=1, source_target_pairs={{0,8},{1,9},{2,10},{3,11},{4,12},{5,13},{6,14},{7,15},{8,0},{9,1},... | collective-permute-start | bytes 4718600 | tf_op jit(solution)/shard_map/ppermute | solution.py:43
  2.1 19.3 %collective-permute-start.7 = (bf16[128,3072]{1,0:T(8,128)(2,1)}, bf16[128,3072]{1,0:T(8,128)(2,1)S(1)}, u32[]{:S(2)}, u32[]{:S(2)}) collective-permute-start(bf16[128,3072]{1,0:T(8,128)(2,1)} %bitcast.21), channel_id=1, source_target_pairs={{0,1},{1,0},{2,3},{3,2},{4,5},{5,4},{6,7},{7,6},{8,9},{9,8},{10,11... | collective-permute-start | bytes 2359304 | tf_op jit(solution)/shard_map/ppermute | solution.py:43
  3.4 21.8 %collective-permute-start.6 = (bf16[128,3072]{1,0:T(8,128)(2,1)}, bf16[128,3072]{1,0:T(8,128)(2,1)S(1)}, u32[]{:S(2)}, u32[]{:S(2)}) collective-permute-start(bf16[128,3072]{1,0:T(8,128)(2,1)} %bitcast.22), channel_id=1, source_target_pairs={{0,6},{1,7},{2,0},{3,1},{4,2},{5,3},{6,4},{7,5},{8,14},{9,15},{10,... | collective-permute-start | bytes 2359304 | tf_op jit(solution)/shard_map/ppermute | solution.py:43
  6.2 27.0 %collective-permute-start.5 = (bf16[128,3072]{1,0:T(8,128)(2,1)}, bf16[128,3072]{1,0:T(8,128)(2,1)S(1)}, u32[]{:S(2)}, u32[]{:S(2)}) collective-permute-start(bf16[128,3072]{1,0:T(8,128)(2,1)} %bitcast.23), channel_id=1, source_target_pairs={{0,2},{1,3},{2,4},{3,5},{4,6},{5,7},{6,0},{7,1},{8,10},{9,11},{10,... | collective-permute-start | bytes 2359304 | tf_op jit(solution)/shard_map/ppermute | solution.py:43
  6.9 26.4 %slice-start = ((s8[9437184]{0:T(1024)(128)(4,1)}), s8[4194304]{0:T(1024)(128)(4,1)S(1)}, s32[]{:S(2)}) async-start(s8[9437184]{0:T(1024)(128)(4,1)} %bitcast.13), calls=%async_computation | async-start | bytes 8388608
  6.9 26.4 %slice-start.1 = ((s8[9437184]{0:T(1024)(128)(4,1)}), s8[4194304]{0:T(1024)(128)(4,1)S(1)}, s32[]{:S(2)}) async-start(s8[9437184]{0:T(1024)(128)(4,1)} %bitcast.13), calls=%async_computation.1 | async-start | bytes 8388608
  11.0 22.2 %slice-start.2 = ((s8[9437184]{0:T(1024)(128)(4,1)}), s8[1048576]{0:T(1024)(128)(4,1)S(1)}, s32[]{:S(2)}) async-start(s8[9437184]{0:T(1024)(128)(4,1)} %bitcast.13), calls=%async_computation.2 | async-start | bytes 2097152
  14.5 18.7 %copy-start.2 = (bf16[1,128,3072]{2,1,0:T(8,128)(2,1)S(1)}, bf16[1,128,3072]{2,1,0:T(8,128)(2,1)}, u32[]{:S(2)}) copy-start(bf16[1,128,3072]{2,1,0:T(8,128)(2,1)} %param.10) | copy-start | bytes 2359300
  14.5 14.1 %collective-permute-start.1 = (bf16[2,16,3072]{2,1,0:T(8,128)(2,1)S(1)}, bf16[2,16,3072]{2,1,0:T(8,128)(2,1)S(1)}, u32[]{:S(2)}, u32[]{:S(2)}) collective-permute-start(bf16[2,16,3072]{2,1,0:T(8,128)(2,1)S(1)} %get-tuple-element.28), channel_id=1, source_target_pairs={{0,16},{1,17},{2,18},{3,19},{4,20},{5,21},{6,22},{7,23},{8,24},{9,... | collective-permute-start | bytes 589832 | tf_op jit(solution)/shard_map/ppermute | solution.py:43
  16.3 13.6 %collective-permute-start.2 = (bf16[2,16,3072]{2,1,0:T(8,128)(2,1)S(1)}, bf16[2,16,3072]{2,1,0:T(8,128)(2,1)S(1)}, u32[]{:S(2)}, u32[]{:S(2)}) collective-permute-start(bf16[2,16,3072]{2,1,0:T(8,128)(2,1)S(1)} %get-tuple-element.29), channel_id=1, source_target_pairs={{0,32},{1,33},{2,34},{3,35},{4,36},{5,37},{6,38},{7,39},{8,40},{9,... | collective-permute-start | bytes 589832 | tf_op jit(solution)/shard_map/ppermute | solution.py:43
  21.4 8.4 %collective-permute-start.3 = (bf16[2,16,3072]{2,1,0:T(8,128)(2,1)S(1)}, bf16[2,16,3072]{2,1,0:T(8,128)(2,1)S(1)}, u32[]{:S(2)}, u32[]{:S(2)}) collective-permute-start(bf16[2,16,3072]{2,1,0:T(8,128)(2,1)S(1)} %get-tuple-element.30), channel_id=1, source_target_pairs={{0,48},{1,49},{2,50},{3,51},{4,52},{5,53},{6,54},{7,55},{8,56},{9,... | collective-permute-start | bytes 589832 | tf_op jit(solution)/shard_map/ppermute | solution.py:43
  25.8 28.8 %collective-permute-start.11 = (bf16[128,3072]{1,0:T(8,128)(2,1)S(1)}, bf16[128,3072]{1,0:T(8,128)(2,1)S(1)}, u32[]{:S(2)}, u32[]{:S(2)}) collective-permute-start(bf16[128,3072]{1,0:T(8,128)(2,1)S(1)} %get-tuple-element.33.refs_2_), channel_id=1, source_target_pairs={{0,6},{1,7},{2,0},{3,1},{4,2},{5,3},{6,4},{7,5},{8,14},{9,15},{10,... | collective-permute-start | bytes 2359304 | tf_op jit(solution)/shard_map/ppermute | solution.py:43
  28.6 20.8 %collective-permute-start.9 = (bf16[128,3072]{1,0:T(8,128)(2,1)S(1)}, bf16[128,3072]{1,0:T(8,128)(2,1)S(1)}, u32[]{:S(2)}, u32[]{:S(2)}) collective-permute-start(bf16[128,3072]{1,0:T(8,128)(2,1)S(1)} %get-tuple-element.33.refs_2_), channel_id=1, source_target_pairs={{0,1},{1,0},{2,3},{3,2},{4,5},{5,4},{6,7},{7,6},{8,9},{9,8},{10,11... | collective-permute-start | bytes 2359304 | tf_op jit(solution)/shard_map/ppermute | solution.py:43
  29.9 19.5 %collective-permute-start.10 = (bf16[128,3072]{1,0:T(8,128)(2,1)S(1)}, bf16[128,3072]{1,0:T(8,128)(2,1)S(1)}, u32[]{:S(2)}, u32[]{:S(2)}) collective-permute-start(bf16[128,3072]{1,0:T(8,128)(2,1)S(1)} %get-tuple-element.34.refs_3_), channel_id=1, source_target_pairs={{0,2},{1,3},{2,4},{3,5},{4,6},{5,7},{6,0},{7,1},{8,10},{9,11},{10,... | collective-permute-start | bytes 2359304 | tf_op jit(solution)/shard_map/ppermute | solution.py:43
  30.5 22.3 %collective-permute-start.4 = (f32[16,3072]{1,0:T(8,128)S(1)}, f32[16,3072]{1,0:T(8,128)S(1)}, u32[]{:S(2)}, u32[]{:S(2)}) collective-permute-start(f32[16,3072]{1,0:T(8,128)S(1)} %get-tuple-element.32), channel_id=1, source_target_pairs={{0,64},{1,65},{2,66},{3,67},{4,68},{5,69},{6,70},{7,71},{8,72},{9,... | collective-permute-start | bytes 589832 | tf_op jit(solution)/shard_map/ppermute | solution.py:43
  49.4 3.4 %copy-start = (bf16[1,256,3072]{2,1,0:T(8,128)(2,1)S(1)}, bf16[1,256,3072]{2,1,0:T(8,128)(2,1)}, u32[]{:S(2)}) copy-start(bf16[1,256,3072]{2,1,0:T(8,128)(2,1)} %param.7) | copy-start | bytes 4718596
  49.4 3.4 %copy-start.1 = (f32[1,16,3072]{2,1,0:T(8,128)S(1)}, f32[1,16,3072]{2,1,0:T(8,128)}, u32[]{:S(2)}) copy-start(f32[1,16,3072]{2,1,0:T(8,128)} %param.9) | copy-start | bytes 589828
  50.0 13.8 %collective-permute-start.15 = (bf16[128,3072]{1,0:T(8,128)(2,1)S(1)}, bf16[128,3072]{1,0:T(8,128)(2,1)S(1)}, u32[]{:S(2)}, u32[]{:S(2)}) collective-permute-start(bf16[128,3072]{1,0:T(8,128)(2,1)S(1)} %pick.1), channel_id=1, source_target_pairs={{0,2},{1,3},{2,4},{3,5},{4,6},{5,7},{6,0},{7,1},{8,14},{9,15},{10,... | collective-permute-start | bytes 2359304 | tf_op jit(solution)/shard_map/ppermute | solution.py:43
  54.1 5.7 %collective-permute-start.8 = (bf16[16,3072]{1,0:T(8,128)(2,1)S(1)}, bf16[16,3072]{1,0:T(8,128)(2,1)S(1)}, u32[]{:S(2)}, u32[]{:S(2)}) collective-permute-start(bf16[16,3072]{1,0:T(8,128)(2,1)S(1)} %get-tuple-element.39.refs_6_.refs_0_), channel_id=1, source_target_pairs={{0,64},{1,65},{2,66},{3,67},{4,68},{5,69},{6,70},{7,71},{8,72},{9,... | collective-permute-start | bytes 294920 | tf_op jit(solution)/shard_map/ppermute | solution.py:43
  60.4 12.0 %collective-permute-start.14 = (bf16[2,16,3072]{2,1,0:T(8,128)(2,1)S(1)}, bf16[2,16,3072]{2,1,0:T(8,128)(2,1)S(1)}, u32[]{:S(2)}, u32[]{:S(2)}) collective-permute-start(bf16[2,16,3072]{2,1,0:T(8,128)(2,1)S(1)} %stack.2.refs_4_.refs_0_), channel_id=1, source_target_pairs={{0,16},{1,17},{2,18},{3,19},{4,20},{5,21},{6,22},{7,23},{8,24},{9,... | collective-permute-start | bytes 589832 | tf_op jit(solution)/shard_map/ppermute | solution.py:43
  60.5 11.9 %collective-permute-start.13 = (bf16[2,16,3072]{2,1,0:T(8,128)(2,1)S(1)}, bf16[2,16,3072]{2,1,0:T(8,128)(2,1)S(1)}, u32[]{:S(2)}, u32[]{:S(2)}) collective-permute-start(bf16[2,16,3072]{2,1,0:T(8,128)(2,1)S(1)} %stack.2.refs_4_.refs_0_), channel_id=1, source_target_pairs={{0,32},{1,33},{2,34},{3,35},{4,36},{5,37},{6,38},{7,39},{8,40},{9,... | collective-permute-start | bytes 589832 | tf_op jit(solution)/shard_map/ppermute | solution.py:43
  63.8 8.6 %collective-permute-start.12 = (bf16[2,16,3072]{2,1,0:T(8,128)(2,1)S(1)}, bf16[2,16,3072]{2,1,0:T(8,128)(2,1)S(1)}, u32[]{:S(2)}, u32[]{:S(2)}) collective-permute-start(bf16[2,16,3072]{2,1,0:T(8,128)(2,1)S(1)} %stack.2.refs_4_.refs_0_), channel_id=1, source_target_pairs={{0,48},{1,49},{2,50},{3,51},{4,52},{5,53},{6,54},{7,55},{8,56},{9,... | collective-permute-start | bytes 589832 | tf_op jit(solution)/shard_map/ppermute | solution.py:43
  73.0 8.0 %collective-permute-start.16 = (bf16[4,2,16,3072]{3,2,1,0:T(8,128)(2,1)S(1)}, bf16[4,2,16,3072]{3,2,1,0:T(8,128)(2,1)S(1)}, u32[]{:S(2)}, u32[]{:S(2)}) collective-permute-start(bf16[4,2,16,3072]{3,2,1,0:T(8,128)(2,1)S(1)} %stack.3.refs_4_.refs_0_), channel_id=1, source_target_pairs={{0,8},{1,9},{2,10},{3,11},{4,12},{5,13},{6,14},{7,15},{8,0},{9,1},... | collective-permute-start | bytes 2359304 | tf_op jit(solution)/shard_map/ppermute | solution.py:43
